TPU v7x, 32 devices: a whole 2x2x4 slice. The times are simulated.
32 devices in a mesh: tile: 16 (over z, y, x), narrow: 2 (over core).
Axes of the slice: x: 2, y: 2, z: 4, core: 2. Of those that a mesh axis runs over, the one named last changes fastest.
Arguments:
- fine: bfloat16 [256, 16, 512], P('tile', 'narrow'), may hold values from -6 to 6
- coarse: bfloat16 [64, 128, 1024], P('tile'), may hold values from -6 to 6
- block_table: int32 [16, 8], P('tile'), may hold values from 0 to 63, as said below
- shifts: int32 [2], replicated, may hold values from 1 to 7
- attn_gain: float32 [512], replicated, may hold values from 0.1 to 1.9
- w_query: bfloat16 [512, 512], replicated, may hold values from -8 to 8
- w_key: bfloat16 [512, 512], replicated, may hold values from -8 to 8
- w_value: bfloat16 [512, 512], replicated, may hold values from -0.25 to 0.25
- w_out: bfloat16 [512, 512], replicated, may hold values from -0.25 to 0.25
- coarse_key: bfloat16 [1024, 512], replicated, may hold values from -0.1875 to 0.1875
- coarse_value: bfloat16 [1024, 512], replicated, may hold values from -0.1875 to 0.1875
- mlp_gain: float32 [512], replicated, may hold values from 0.1 to 1.9
- w_gate: bfloat16 [512, 2048], replicated, may hold values from -0.25 to 0.25
- w_up: bfloat16 [512, 2048], replicated, may hold values from -0.25 to 0.25
- w_down: bfloat16 [2048, 512], replicated, may hold values from -0.125 to 0.125
Outputs:
- output: bfloat16 [256, 16, 512], P('tile', 'narrow')
Inputs may be any that keep to these rules, and one draw needn't show every extreme that they name: `block_table`: row s names 8 distinct blocks, all among blocks (s - 1) * 4 to (s + 2) * 4 - 1 taken modulo 64, at least one of them below s * 4 and at least one at or above (s + 1) * 4 in that range.
All inputs are finite; a program needn't handle non-finite values.
Results may differ from a plain program's by a relative error of at most 0.0073.
Values may be sent and summed in bfloat16 or wider, within the bound.
A program may use at most 64 MiB of HBM per device.

v0:
```python
import jax
import jax.numpy as jnp
from jax import lax
from jax.sharding import PartitionSpec as P

HEADS = 8
CW = 1024
WS = 8
HD = 64


def passed_along(x, axis, by):
    count = lax.axis_size(axis)
    return lax.ppermute(x, axis, [(i, (i + by) % count) for i in range(count)])


def with_halo(x, sides, width):
    for axis, dim in sides:
        count, length = (lax.axis_size(axis), x.shape[dim])
        up = [(i, (i + 1) % count) for i in range(count)]
        down = [(j, i) for i, j in up]
        last = lax.slice_in_dim(x, length - width, length, axis=dim)
        initial = lax.slice_in_dim(x, 0, width, axis=dim)
        before = lax.ppermute(last, axis, up)
        after = lax.ppermute(initial, axis, down)
        x = jnp.concatenate([before, x, after], axis=dim)
    return x


def rms_scale(source, gain_vec):
    values = source.astype(jnp.float32)
    mean_square = jnp.mean(values * values, axis=-1, keepdims=True)
    return values * lax.rsqrt(mean_square + 1e-06) * gain_vec


def to_windows(source):
    lead_count = source.shape[0] // WS
    across = source.shape[1] // WS
    reordered = source.reshape((lead_count, WS, across, WS) + source.shape[2:])
    reordered = jnp.swapaxes(reordered, 1, 2)
    return reordered.reshape((lead_count * across, WS * WS) + source.shape[2:])


def from_windows(source, row_count, column_count):
    reordered = source.reshape((row_count // WS, column_count // WS, WS, WS) + source.shape[2:])
    reordered = jnp.swapaxes(reordered, 1, 2)
    return reordered.reshape((row_count, column_count) + source.shape[2:])


def attend(queries, keys_fine, values_fine, coarse_keys, coarse_values, row_flag, column_flag):
    row_count, column_count = (queries.shape[0], queries.shape[1])
    labels = row_flag.astype(jnp.int32)[:, None] * 2 + column_flag.astype(jnp.int32)[None, :]
    labels = to_windows(labels)
    allowed = labels[:, :, None] == labels[:, None, :]
    query_win = to_windows(queries)
    key_win = to_windows(keys_fine)
    value_win = to_windows(values_fine)
    score_self = jnp.einsum(
        "wqhd,wkhd->whqk", query_win, key_win, preferred_element_type=jnp.float32
    )
    score_self = jnp.where(allowed[:, None], score_self, -jnp.inf)
    score_cross = jnp.einsum(
        "wqhd,khd->whqk", query_win, coarse_keys, preferred_element_type=jnp.float32
    )
    maxima = jnp.maximum(
        jnp.max(score_self, axis=-1, keepdims=True), jnp.max(score_cross, axis=-1, keepdims=True)
    )
    exp_self = jnp.exp(score_self - maxima)
    exp_cross = jnp.exp(score_cross - maxima)
    totals = jnp.sum(exp_self, axis=-1, keepdims=True) + jnp.sum(exp_cross, axis=-1, keepdims=True)
    prob_self = (exp_self / totals).astype(jnp.bfloat16)
    prob_cross = (exp_cross / totals).astype(jnp.bfloat16)
    mixture = jnp.einsum(
        "whqk,wkhd->wqhd", prob_self, value_win, preferred_element_type=jnp.float32
    )
    mixture = mixture + jnp.einsum(
        "whqk,khd->wqhd", prob_cross, coarse_values, preferred_element_type=jnp.float32
    )
    return from_windows(mixture.astype(jnp.bfloat16), row_count, column_count)


def local(
    fine,
    coarse,
    block_table,
    shifts,
    attn_gain,
    w_query,
    w_key,
    w_value,
    w_out,
    coarse_key,
    coarse_value,
    mlp_gain,
    w_gate,
    w_up,
    w_down,
):
    strip_count = lax.axis_size("tile")
    strip_index = lax.axis_index("tile")
    member_count = lax.axis_size("narrow")
    member_index = lax.axis_index("narrow")
    rows_dev, columns, feature_width = fine.shape
    shift_row = shifts[0]
    shift_col = shifts[1]
    zero_index = jnp.zeros((), jnp.int32)
    right_cols = passed_along(fine, "narrow", -1)
    widened = jnp.concatenate([fine, right_cols], axis=1)
    lower_rows = passed_along(widened[:WS], "tile", -1)
    extended = jnp.concatenate([widened, lower_rows], axis=0)
    rolled = lax.dynamic_slice(
        extended, (shift_row, shift_col, zero_index), (rows_dev, columns, feature_width)
    )
    flat_rows = rolled.reshape(-1, feature_width)
    normed = rms_scale(flat_rows, attn_gain).astype(jnp.bfloat16)
    query_scale = 1.0 / HD**0.5
    queries = (jnp.dot(normed, w_query, preferred_element_type=jnp.float32) * query_scale).astype(
        jnp.bfloat16
    )
    keys_fine = jnp.dot(normed, w_key, preferred_element_type=jnp.float32).astype(jnp.bfloat16)
    values_fine = jnp.dot(normed, w_value, preferred_element_type=jnp.float32).astype(jnp.bfloat16)
    queries = queries.reshape(rows_dev, columns, HEADS, HD)
    keys_fine = keys_fine.reshape(rows_dev, columns, HEADS, HD)
    values_fine = values_fine.reshape(rows_dev, columns, HEADS, HD)
    blocks_dev = coarse.shape[0]
    total_blocks = blocks_dev * strip_count
    local_index = jnp.mod(block_table[0] - (strip_index - 1) * blocks_dev, total_blocks)
    nearby = with_halo(coarse, (("tile", 0),), blocks_dev)
    chosen = jnp.take(nearby, local_index, axis=0).reshape(-1, CW)
    coarse_keys = jnp.dot(chosen, coarse_key, preferred_element_type=jnp.float32).astype(
        jnp.bfloat16
    )
    coarse_values = jnp.dot(chosen, coarse_value, preferred_element_type=jnp.float32).astype(
        jnp.bfloat16
    )
    coarse_keys = coarse_keys.reshape(-1, HEADS, HD)
    coarse_values = coarse_values.reshape(-1, HEADS, HD)
    row_total = rows_dev * strip_count
    column_total = columns * member_count
    row_flag = (
        strip_index * rows_dev + jnp.arange(rows_dev, dtype=jnp.int32) + shift_row >= row_total
    )
    column_flag = (
        member_index * columns + jnp.arange(columns, dtype=jnp.int32) + shift_col >= column_total
    )
    head_out = attend(
        queries, keys_fine, values_fine, coarse_keys, coarse_values, row_flag, column_flag
    )
    attn_sum = jnp.dot(
        head_out.reshape(-1, feature_width), w_out, preferred_element_type=jnp.float32
    )
    mid = flat_rows.astype(jnp.float32) + attn_sum
    normed_mid = rms_scale(mid, mlp_gain).astype(jnp.bfloat16)
    gate_term = jnp.dot(normed_mid, w_gate, preferred_element_type=jnp.float32)
    up_term = jnp.dot(normed_mid, w_up, preferred_element_type=jnp.float32)
    hidden = (jax.nn.silu(gate_term) * up_term).astype(jnp.bfloat16)
    mlp_sum = jnp.dot(hidden, w_down, preferred_element_type=jnp.float32)
    block_out = (mid + mlp_sum).astype(jnp.bfloat16).reshape(rows_dev, columns, feature_width)
    left_cols = passed_along(block_out, "narrow", 1)
    widened_out = jnp.concatenate([left_cols, block_out], axis=1)
    upper_rows = passed_along(widened_out[rows_dev - WS :], "tile", 1)
    joined = jnp.concatenate([upper_rows, widened_out], axis=0)
    return lax.dynamic_slice(
        joined, (WS - shift_row, WS - shift_col, zero_index), (rows_dev, columns, feature_width)
    )


def solution(mesh):
    placed = (
        P("tile", "narrow", None),
        P("tile", None, None),
        P("tile", None),
        P(),
        P(),
        P(),
        P(),
        P(),
        P(),
        P(),
        P(),
        P(),
        P(),
        P(),
        P(),
    )
    return jax.shard_map(
        local, mesh=mesh, in_specs=placed, out_specs=P("tile", "narrow", None), check_vma=False
    )
```

profile of v0, /device:TPU:0, one launch (start us, length us, event | category | flops | bytes accessed | tf_op | source)
XLA Modules:
  0.0 106.3 jit_solution(12168193709016859154)
XLA Ops:
  0.0 0.0 copy-start
  0.0 2.9 %collective-permute-start.2 = (bf16[4,128,1024]{2,1,0:T(8,128)(2,1)}, bf16[4,128,1024]{2,1,0:T(8,128)(2,1)}, u32[]{:S(2)}, u32[]{:S(2)}) collective-permute-start(bf16[4,128,1024]{2,1,0:T(8,128)(2,1)} %param.16), channel_id=1, source_target_pairs={{0,2},{2,4},{4,6},{6,8},{8,10},{10,12},{12,14},{14,16},{16,18},{18... | collective-permute-start | bytes 3145736 | tf_op jit(solution)/shard_map/ppermute | solution.py:24
  2.9 4.1 %collective-permute-start.3 = (bf16[4,128,1024]{2,1,0:T(8,128)(2,1)}, bf16[4,128,1024]{2,1,0:T(8,128)(2,1)}, u32[]{:S(2)}, u32[]{:S(2)}) collective-permute-start(bf16[4,128,1024]{2,1,0:T(8,128)(2,1)} %param.16), channel_id=1, source_target_pairs={{2,0},{4,2},{6,4},{8,6},{10,8},{12,10},{14,12},{16,14},{18,16},{20... | collective-permute-start | bytes 3145736 | tf_op jit(solution)/shard_map/ppermute | solution.py:25
  7.0 0.0 collective-permute-start
  7.0 1.4 %fusion.52 = (s32[1]{0:T(128)}, s32[1]{0:T(128)}) fusion(s32[2]{0:T(128)} %param.18), kind=kLoop, calls=%fused_computation.87 | loop fusion | bytes 16 | tf_op jit(solution)/shard_map/slice | solution.py:105
  8.4 0.7 compare_convert_fusion
  9.1 0.1 add.167
  9.2 0.6 compare_select_fusion.6
  9.8 0.1 add.160
  9.9 0.1 add.161
  10.0 0.7 broadcast_compare_fusion
  10.7 0.7 compare_and_fusion
  11.3 0.1 broadcast_bitcast_fusion
  11.4 0.9 constant_dynamic-update-slice_fusion.1
  12.3 0.0 collective-permute-done
  12.4 2.0 %collective-permute-start.1 = (bf16[8,16,512]{2,1,0:T(8,128)(2,1)S(1)}, bf16[8,16,512]{2,1,0:T(8,128)(2,1)S(1)}, u32[]{:S(2)}, u32[]{:S(2)}) collective-permute-start(bf16[8,16,512]{2,1,0:T(8,128)(2,1)S(1)} %slice.18), channel_id=1, source_target_pairs={{0,30},{2,0},{4,2},{6,4},{8,6},{10,8},{12,10},{14,12},{16,14},{18,... | collective-permute-start | bytes 393224 | tf_op jit(solution)/shard_map/ppermute | solution.py:14
  14.4 0.7 fusion.46
  19.0 33.8 %collective-permute-done.1 = bf16[8,16,512]{2,1,0:T(8,128)(2,1)S(1)} collective-permute-done((bf16[8,16,512]{2,1,0:T(8,128)(2,1)S(1)}, bf16[8,16,512]{2,1,0:T(8,128)(2,1)S(1)}, u32[]{:S(2)}, u32[]{:S(2)}) %collective-permute-start.1) | collective-permute-done | bytes 131104 | tf_op jit(solution)/shard_map/ppermute | solution.py:14
  52.8 0.3 fusion.28
  53.1 0.1 rsqrt.20
  53.2 2.0 %fusion.15 = bf16[128,512]{1,0:T(8,128)(2,1)} fusion(bf16[512,512]{1,0:T(8,128)(2,1)} %param.20, bf16[16,8,512]{2,1,0:T(8,128)(2,1)S(1)} %get-tuple-element.6, f32[512]{0:T(512)} %param.19, f32[128]{0:T(128)S(1)} %rsqrt.20), kind=kOutput, calls=%fused_computation.21 | convolution fusion | flops 67502080 | bytes 788992 | tf_op jit(solution)/shard_map/dot_general | solution.py:117
  55.2 1.2 %reshape_transpose_reshape_reshape.10 = bf16[2,64,8,64]{3,2,1,0:T(8,128)(2,1)S(1)} reshape(bf16[128,512]{1,0:T(8,128)(2,1)} %fusion.15) | data formatting | bytes 262144 | tf_op jit(solution)/shard_map/reshape;transpose;reshape;reshape | solution.py:41
  56.4 0.0 copy-done.7
  56.4 2.0 %convolution_convert_fusion.3 = bf16[128,512]{1,0:T(8,128)(2,1)} fusion(bf16[512,512]{1,0:T(8,128)(2,1)} %param.22, bf16[16,8,512]{2,1,0:T(8,128)(2,1)S(1)} %get-tuple-element.6, f32[512]{0:T(512)S(1)} %copy-done.7, f32[128]{0:T(128)S(1)} %rsqrt.20), kind=kOutput, calls=%fused_computation.23 | convolution fusion | flops 67436544 | bytes 788992 | tf_op jit(solution)/shard_map/dot_general | solution.py:121
  58.3 1.8 %reshape_transpose_reshape_reshape.9 = bf16[2,64,8,64]{3,2,1,0:T(8,128)(2,1)} reshape(bf16[128,512]{1,0:T(8,128)(2,1)} %convolution_convert_fusion.3) | data formatting | bytes 262144 | tf_op jit(solution)/shard_map/reshape;transpose;reshape;reshape | solution.py:41
  60.1 2.0 %convolution_convert_fusion.2 = bf16[128,512]{1,0:T(8,128)(2,1)} fusion(bf16[512,512]{1,0:T(8,128)(2,1)} %param.21, bf16[16,8,512]{2,1,0:T(8,128)(2,1)S(1)} %get-tuple-element.6, f32[512]{0:T(512)S(1)} %copy-done.7, f32[128]{0:T(128)S(1)} %rsqrt.20), kind=kOutput, calls=%fused_computation.22 | convolution fusion | flops 67436544 | bytes 788992 | tf_op jit(solution)/shard_map/dot_general | solution.py:120
  62.1 1.8 %reshape_transpose_reshape_reshape.11 = bf16[2,64,8,64]{3,2,1,0:T(8,128)(2,1)} reshape(bf16[128,512]{1,0:T(8,128)(2,1)} %convolution_convert_fusion.2) | data formatting | bytes 262144 | tf_op jit(solution)/shard_map/reshape;transpose;reshape;reshape | solution.py:41
  63.9 0.8 copy.44
  64.7 2.0 %fusion.53 = (f32[2,8,64]{2,1,0:T(8,128)S(1)}, f32[2,8,64,64]{2,3,1,0:T(8,128)}) fusion(bf16[2,64,8,64]{3,2,1,0:T(8,128)(2,1)} %reshape_transpose_reshape_reshape.11, bf16[2,64,8,64]{3,2,1,0:T(8,128)(2,1)S(1)} %reshape_transpose_reshape_reshape.10, pred[2,64,64]{1,2,0:T(8,128)(4,1)} %broadcast_compare_fusion), kind=kOutput, calls=%fused_computation.88 | convolution fusion | flops 8518656 | bytes 536576 | tf_op jit(solution)/shard_map/wqhd,wkhd->whqk/dot_general | solution.py:58
  66.7 0.0 collective-permute-done.2
  66.7 0.0 collective-permute-done.3
  66.7 0.0 copy-done.2
  66.7 3.1 %pad_maximum_fusion = bf16[12,128,1024]{2,1,0:T(8,128)(2,1)} fusion(bf16[4,128,1024]{2,1,0:T(8,128)(2,1)} %collective-permute-done.3, bf16[4,128,1024]{2,1,0:T(8,128)(2,1)S(1)} %copy-done.2, bf16[4,128,1024]{2,1,0:T(8,128)(2,1)} %collective-permute-done.2), kind=kLoop, calls=%fused_computation.4 | loop fusion | flops 3145728 | bytes 6291456 | tf_op jit(solution)/shard_map/concatenate | solution.py:26
  69.8 3.9 %gather_fusion = bf16[8,128,1024]{2,1,0:T(8,128)(2,1)} fusion(bf16[12,128,1024]{2,1,0:T(8,128)(2,1)} %pad_maximum_fusion, s32[1024]{0:T(1024)S(1)} %pad_clamp_fusion), kind=kCustom, calls=%fused_computation | custom fusion | bytes 4194336 | tf_op jit(solution)/shard_map/jit(_take)/gather | solution.py:129
  73.7 1.9 %bitcast_select_fusion = bf16[1024,1024]{1,0:T(8,128)(2,1)S(1)} fusion(bf16[8,128,1024]{2,1,0:T(8,128)(2,1)} %gather_fusion, pred[1024]{0:T(1024)(128)(4,1)S(1)} %broadcast_bitcast_fusion), kind=kLoop, calls=%fused_computation.7 | loop fusion | flops 1048576 | bytes 4195328 | tf_op jit(solution)/shard_map/jit(_take)/select_n | solution.py:129
  75.6 0.0 copy-done.9
  75.6 0.0 copy-start.10
  75.7 2.3 %convolution_convert_fusion = bf16[1024,512]{0,1:T(8,128)(2,1)} fusion(bf16[1024,1024]{1,0:T(8,128)(2,1)S(1)} %bitcast_select_fusion, bf16[1024,512]{1,0:T(8,128)(2,1)S(1)} %copy-done.9), kind=kOutput, calls=%fused_computation.10 | convolution fusion | flops 1074266112 | bytes 4194304 | tf_op jit(solution)/shard_map/dot_general | solution.py:133
  78.0 0.0 copy-done.10
  78.0 1.3 %convolution_convert_fusion.1 = bf16[1024,512]{0,1:T(8,128)(2,1)S(1)} fusion(bf16[1024,1024]{1,0:T(8,128)(2,1)S(1)} %bitcast_select_fusion, bf16[1024,512]{1,0:T(8,128)(2,1)S(1)} %copy-done.10), kind=kOutput, calls=%fused_computation.11 | convolution fusion | flops 1074266112 | bytes 4194304 | tf_op jit(solution)/shard_map/dot_general | solution.py:130
  79.3 0.0 copy-done.3
  79.3 2.6 %fusion.54 = f32[8,1024,128]{1,2,0} fusion(bf16[8,64,128]{1,2,0:T(8,128)(2,1)S(1)} %bitcast.68, bf16[1024,8,64]{0,2,1:T(8,128)(2,1)S(1)} %bitcast.67), kind=kOutput, calls=%fused_computation.89 | convolution fusion | flops 134217728 | bytes 5373952
  81.9 2.5 %reduce_max.19 = f32[2,8,64]{2,0,1:T(2,128)S(1)} reduce(f32[2,8,64,1024]{3,2,0,1:T(8,128)} %bitcast.65, f32[]{:T(128)} %constant.67.clone.1), dimensions={3}, to_apply=%region_2.3 | reduce | flops 1047552 | bytes 4198404 | tf_op jit(solution)/shard_map/reduce_max | solution.py:66
  84.5 0.0 copy-start.6
  84.5 0.0 copy-start.1
  84.5 3.1 %fusion = f32[2,8,64]{2,0,1:T(2,128)S(1)} fusion(f32[2,8,64,1024]{3,2,0,1:T(8,128)} %bitcast.66, f32[2,8,64]{2,0,1:T(2,128)S(1)} %copy.46), kind=kLoop, calls=%fused_computation.3 | loop fusion | flops 2096128 | bytes 4202496 | tf_op jit(solution)/shard_map/reduce_sum | solution.py:70
  87.6 0.0 copy-start.11
  87.6 0.0 copy-done.4
  87.6 0.1 fusion.24
  87.7 0.0 copy-done.6
  87.8 0.3 convolution_bitcast_fusion
  88.0 0.0 copy-done.1
  88.0 0.9 copy-done.11
  88.9 1.5 %fusion.11 = bf16[2,64,8,64]{1,3,2,0:T(8,128)(2,1)S(1)} fusion(f32[2,64,8,64]{1,3,2,0:T(8,128)S(1)} %convolution_bitcast_fusion, bf16[1024,8,64,1]{0,2,1,3:T(8,128)(2,1)S(1)} %bitcast.69, f32[2,8,64]{2,0,1:T(2,128)S(1)} %copy.50, f32[2,8,64]{2,0,1:T(2,128)S(1)} %copy.46, f32[8,1024,128]{1,2,0:S(1)} %copy-done.1), kind=kOutput, calls=%fused_computation.17 | convolution fusion | flops 137494528 | bytes 5644288 | tf_op jit(solution)/shard_map/whqk,khd->wqhd/dot_general | solution.py:76
  90.5 0.2 copy.52
  90.7 0.2 reshape_reshape_transpose_reshape.3
  90.9 0.3 multiply_reduce_fusion
  91.2 0.5 fusion.34
  91.7 3.1 %fusion.17 = bf16[16,8,512]{2,1,0:T(8,128)(2,1)S(1)} fusion(f32[128,512]{1,0:T(8,128)S(1)} %get-tuple-element.12, bf16[2048,512]{1,0:T(8,128)(2,1)} %param.29, bf16[512,2048]{1,0:T(8,128)(2,1)} %param.28, f32[128,2048]{1,0:T(8,128)S(1)} %fusion.34, f32[512]{0:T(512)S(1)} %copy-done.8, f32[128]{0:T(128)S(1)} %add_rsqrt_fusion.1), kind=kOutput, calls=%fused_computation.25 | convolution fusion | flops 538771456 | bytes 5638656 | tf_op jit(solution)/shard_map/dot_general | solution.py:157
  94.8 0.1 collective-permute-start.4
  94.9 1.3 %collective-permute-done.4 = bf16[16,8,512]{2,1,0:T(8,128)(2,1)S(1)} collective-permute-done((bf16[16,8,512]{2,1,0:T(8,128)(2,1)S(1)}, bf16[16,8,512]{2,1,0:T(8,128)(2,1)S(1)}, u32[]{:S(2)}, u32[]{:S(2)}) %collective-permute-start.4) | collective-permute-done | bytes 131104 | tf_op jit(solution)/shard_map/ppermute | solution.py:14
  96.2 1.5 %collective-permute-start.5 = (bf16[8,16,512]{2,1,0:T(8,128)(2,1)S(1)}, bf16[8,16,512]{2,1,0:T(8,128)(2,1)S(1)}, u32[]{:S(2)}, u32[]{:S(2)}) collective-permute-start(bf16[8,16,512]{2,1,0:T(8,128)(2,1)S(1)} %pad_maximum_fusion.1), channel_id=1, source_target_pairs={{0,2},{2,4},{4,6},{6,8},{8,10},{10,12},{12,14},{14,16},{16,18},{18... | collective-permute-start | bytes 393224 | tf_op jit(solution)/shard_map/ppermute | solution.py:14
  100.4 5.0 %collective-permute-done.5 = bf16[8,16,512]{2,1,0:T(8,128)(2,1)S(1)} collective-permute-done((bf16[8,16,512]{2,1,0:T(8,128)(2,1)S(1)}, bf16[8,16,512]{2,1,0:T(8,128)(2,1)S(1)}, u32[]{:S(2)}, u32[]{:S(2)}) %collective-permute-start.5) | collective-permute-done | bytes 131104 | tf_op jit(solution)/shard_map/ppermute | solution.py:14
  105.4 0.9 fusion.35
  (22 shorter events, 0.1 us)
Async XLA Ops:
  0.0 91.2 %copy-start = (bf16[512,2048]{1,0:T(8,128)(2,1)S(1)}, bf16[512,2048]{1,0:T(8,128)(2,1)}, u32[]{:S(2)}) copy-start(bf16[512,2048]{1,0:T(8,128)(2,1)} %param.27) | copy-start | bytes 6291460
  0.0 56.4 %copy-start.7 = (f32[512]{0:T(512)S(1)}, f32[512]{0:T(512)}, u32[]{:S(2)}) copy-start(f32[512]{0:T(512)} %param.19) | copy-start | bytes 6148
  0.0 66.7 %collective-permute-start.2 = (bf16[4,128,1024]{2,1,0:T(8,128)(2,1)}, bf16[4,128,1024]{2,1,0:T(8,128)(2,1)}, u32[]{:S(2)}, u32[]{:S(2)}) collective-permute-start(bf16[4,128,1024]{2,1,0:T(8,128)(2,1)} %param.16), channel_id=1, source_target_pairs={{0,2},{2,4},{4,6},{6,8},{8,10},{10,12},{12,14},{14,16},{16,18},{18... | collective-permute-start | bytes 3145736 | tf_op jit(solution)/shard_map/ppermute | solution.py:24
  2.9 63.8 %collective-permute-start.3 = (bf16[4,128,1024]{2,1,0:T(8,128)(2,1)}, bf16[4,128,1024]{2,1,0:T(8,128)(2,1)}, u32[]{:S(2)}, u32[]{:S(2)}) collective-permute-start(bf16[4,128,1024]{2,1,0:T(8,128)(2,1)} %param.16), channel_id=1, source_target_pairs={{2,0},{4,2},{6,4},{8,6},{10,8},{12,10},{14,12},{16,14},{18,16},{20... | collective-permute-start | bytes 3145736 | tf_op jit(solution)/shard_map/ppermute | solution.py:25
  7.0 5.3 %collective-permute-start = (bf16[16,8,512]{2,1,0:T(8,128)(2,1)}, bf16[16,8,512]{2,1,0:T(8,128)(2,1)S(1)}, u32[]{:S(2)}, u32[]{:S(2)}) collective-permute-start(bf16[16,8,512]{2,1,0:T(8,128)(2,1)} %param.15), channel_id=1, source_target_pairs={{0,1},{1,0},{2,3},{3,2},{4,5},{5,4},{6,7},{7,6},{8,9},{9,8},{10,11... | collective-permute-start | bytes 393224 | tf_op jit(solution)/shard_map/ppermute | solution.py:14
  12.4 40.4 %collective-permute-start.1 = (bf16[8,16,512]{2,1,0:T(8,128)(2,1)S(1)}, bf16[8,16,512]{2,1,0:T(8,128)(2,1)S(1)}, u32[]{:S(2)}, u32[]{:S(2)}) collective-permute-start(bf16[8,16,512]{2,1,0:T(8,128)(2,1)S(1)} %slice.18), channel_id=1, source_target_pairs={{0,30},{2,0},{4,2},{6,4},{8,6},{10,8},{12,10},{14,12},{16,14},{18,... | collective-permute-start | bytes 393224 | tf_op jit(solution)/shard_map/ppermute | solution.py:14
  55.2 11.6 %copy-start.2 = (bf16[4,128,1024]{2,1,0:T(8,128)(2,1)S(1)}, bf16[4,128,1024]{2,1,0:T(8,128)(2,1)}, u32[]{:S(2)}) copy-start(bf16[4,128,1024]{2,1,0:T(8,128)(2,1)} %param.16) | copy-start | bytes 3145732
  73.7 2.0 %copy-start.9 = (bf16[1024,512]{1,0:T(8,128)(2,1)S(1)}, bf16[1024,512]{1,0:T(8,128)(2,1)}, u32[]{:S(2)}) copy-start(bf16[1024,512]{1,0:T(8,128)(2,1)} %param.25) | copy-start | bytes 3145732
  75.6 2.3 %copy-start.10 = (bf16[1024,512]{1,0:T(8,128)(2,1)S(1)}, bf16[1024,512]{1,0:T(8,128)(2,1)}, u32[]{:S(2)}) copy-start(bf16[1024,512]{1,0:T(8,128)(2,1)} %param.24) | copy-start | bytes 3145732
  78.0 1.3 %copy-start.3 = (bf16[2,64,8,64]{3,1,0,2:T(8,128)(2,1)S(1)}, bf16[2,64,8,64]{3,1,0,2:T(8,128)(2,1)}, u32[]{:S(2)}) copy-start(bf16[2,64,8,64]{3,1,0,2:T(8,128)(2,1)} %copy.44) | copy-start | bytes 393220
  81.9 5.7 %copy-start.4 = (f32[2,8,64,64]{2,3,1,0:T(8,128)S(1)}, f32[2,8,64,64]{2,3,1,0:T(8,128)}, u32[]{:S(2)}) copy-start(f32[2,8,64,64]{2,3,1,0:T(8,128)} %get-tuple-element.10) | copy-start | bytes 786436
  84.5 3.3 %copy-start.6 = (bf16[2,64,8,64]{3,2,1,0:T(8,128)(2,1)S(1)}, bf16[2,64,8,64]{3,2,1,0:T(8,128)(2,1)}, u32[]{:S(2)}) copy-start(bf16[2,64,8,64]{3,2,1,0:T(8,128)(2,1)} %reshape_transpose_reshape_reshape.9) | copy-start | bytes 393220
  84.5 3.5 %copy-start.1 = (f32[8,1024,128]{1,2,0:S(1)}, f32[8,1024,128]{1,2,0}, u32[]{:S(2)}) copy-start(f32[8,1024,128]{1,2,0} %fusion.54) | copy-start | bytes 12582916
  87.6 1.3 %copy-start.11 = (bf16[1024,512]{0,1:T(8,128)(2,1)S(1)}, bf16[1024,512]{0,1:T(8,128)(2,1)}, u32[]{:S(2)}) copy-start(bf16[1024,512]{0,1:T(8,128)(2,1)} %convolution_convert_fusion) | copy-start | bytes 3145732
  88.9 2.0 %copy-start.5 = (bf16[512,512]{1,0:T(8,128)(2,1)S(1)}, bf16[512,512]{1,0:T(8,128)(2,1)}, u32[]{:S(2)}) copy-start(bf16[512,512]{1,0:T(8,128)(2,1)} %param.23) | copy-start | bytes 1572868
  88.9 2.3 %copy-start.8 = (f32[512]{0:T(512)S(1)}, f32[512]{0:T(512)}, u32[]{:S(2)}) copy-start(f32[512]{0:T(512)} %param.26) | copy-start | bytes 6148
  94.8 1.4 %collective-permute-start.4 = (bf16[16,8,512]{2,1,0:T(8,128)(2,1)S(1)}, bf16[16,8,512]{2,1,0:T(8,128)(2,1)S(1)}, u32[]{:S(2)}, u32[]{:S(2)}) collective-permute-start(bf16[16,8,512]{2,1,0:T(8,128)(2,1)S(1)} %fusion.17), channel_id=1, source_target_pairs={{0,1},{1,0},{2,3},{3,2},{4,5},{5,4},{6,7},{7,6},{8,9},{9,8},{10,11... | collective-permute-start | bytes 393224 | tf_op jit(solution)/shard_map/ppermute | solution.py:14
  96.2 9.2 %collective-permute-start.5 = (bf16[8,16,512]{2,1,0:T(8,128)(2,1)S(1)}, bf16[8,16,512]{2,1,0:T(8,128)(2,1)S(1)}, u32[]{:S(2)}, u32[]{:S(2)}) collective-permute-start(bf16[8,16,512]{2,1,0:T(8,128)(2,1)S(1)} %pad_maximum_fusion.1), channel_id=1, source_target_pairs={{0,2},{2,4},{4,6},{6,8},{8,10},{10,12},{12,14},{14,16},{16,18},{18... | collective-permute-start | bytes 393224 | tf_op jit(solution)/shard_map/ppermute | solution.py:14
where the time goes:
time: 107 us; the launch traced here: 106 us
  waiting for transfers between devices  40.2 us (38%)
  matrix products  19.9 us (19%)
  other arithmetic  15.2 us (14%)
  local copies, waits for them, and re-layouts  13.5 us (13%)
  starting transfers between devices  10.6 us (10%)
  between operations  6.86 us (6%)
    ppermute x4, waiting for transfers between devices, passed_along(): return lax.ppermute(x, axis, [(i, (i + by) % count) for i in range(count)])  40.1 us
    another operation x4, local copies, waits for them, and re-layouts, to_windows(): return reordered.reshape((lead_count * across, WS * WS) + source.shape[2:])  5.55 us
    ppermute x1, starting transfers between devices, with_halo(): after = lax.ppermute(initial, axis, down)  4.06 us
    gather x1, local copies, waits for them, and re-layouts, local(): chosen = jnp.take(nearby, local_index, axis=0).reshape(-1, CW)  3.91 us
    ppermute x4, starting transfers between devices, passed_along(): return lax.ppermute(x, axis, [(i, (i + by) % count) for i in range(count)])  3.63 us
    dot_general x1, matrix products, local(): mlp_sum = jnp.dot(hidden, w_down, preferred_element_type=jnp.float32)  3.09 us
    reduce_sum x1, other arithmetic, attend(): jnp.sum(exp_cross, axis=-1, keepdims=True)  3.07 us
    concatenate x1, other arithmetic, with_halo(): x = jnp.concatenate([before, x, after], axis=dim)  3.05 us
  transfers between devices with their start and end apart: 6, of which 3 were waited for; matrix products, arithmetic and copies ran while one was open for 19% of the time, Pallas kernels for 0%

commit v1 on v0

v1 whole, which is shorter than its diff:
```python
import functools

import jax
import jax.numpy as jnp
from jax import lax
from jax.experimental import pallas as pl
from jax.experimental.pallas import tpu as pltpu
from jax.sharding import PartitionSpec as P

WS = 8
HD = 64
HEADS = 8
PAIR = 2 * HD
CT = 128
NB = 8
HIDDEN = -1e30
MESH = pl.DeviceIdType.MESH
F32 = jnp.float32
BF16 = jnp.bfloat16


def dot(a, b):
    return jnp.dot(a, b, preferred_element_type=F32)


def rms_scale(values, gain_vec):
    mean_square = jnp.mean(values * values, axis=-1, keepdims=True)
    return values * lax.rsqrt(mean_square + 1e-06) * gain_vec


def one_hot_rows(index, count):
    lanes = lax.broadcasted_iota(jnp.int32, (index.shape[0], count), 1)
    return (lanes == index).astype(F32).astype(BF16)


def paired(q_t):
    zero = jnp.zeros((HD, q_t.shape[1]), q_t.dtype)
    upper = jnp.concatenate([q_t[:HD], zero], axis=1)
    lower = jnp.concatenate([zero, q_t[HD:]], axis=1)
    return jnp.concatenate([upper, lower], axis=0)


def unpaired(both, tokens):
    return jnp.concatenate([both[:HD, :tokens], both[HD:, tokens:]], axis=0)


def kernel(
    tiles,
    narrows,
    table,
    shifts,
    fine,
    coarse,
    attn_gain,
    w_query,
    w_key,
    w_value,
    w_out,
    coarse_key,
    coarse_value,
    mlp_gain,
    w_gate,
    w_up,
    w_down,
    out,
    ext,
    back,
    coarse_v,
    gain1_v,
    wq_v,
    wk_v,
    wv_v,
    wo_v,
    ck_v,
    cv_v,
    gain2_v,
    wg_v,
    wu_v,
    wd_v,
    keys_v,
    values_t,
    q_send,
    q_from_prev,
    q_from_next,
    o_send,
    st_send,
    o_recv,
    st_recv,
    own_o,
    own_st,
    load_sem,
    send_sem,
    recv_sem,
):
    s = lax.axis_index("tile")
    n = lax.axis_index("narrow")
    s_next, s_prev = lax.rem(s + 1, tiles), lax.rem(s + tiles - 1, tiles)
    n_next, n_prev = lax.rem(n + 1, narrows), lax.rem(n + narrows - 1, narrows)
    tokens, width = fine.shape
    half = WS * WS
    rows_dev = tokens // WS
    blocks = coarse.shape[0] // CT

    barrier = pltpu.get_barrier_semaphore()
    for peer in (
        (s, n_next),
        (s, n_prev),
        (s_next, n),
        (s_prev, n),
        (s_next, n_next),
        (s_prev, n_prev),
    ):
        pl.semaphore_signal(barrier, inc=1, device_id=peer, device_id_type=MESH)

    pairs = (
        (coarse, coarse_v),
        (coarse_key, ck_v),
        (coarse_value, cv_v),
        (fine, ext.at[pl.ds(0, tokens)]),
        (attn_gain, gain1_v),
        (w_query, wq_v),
        (w_key, wk_v),
        (w_value, wv_v),
        (w_out, wo_v),
        (mlp_gain, gain2_v),
        (w_gate, wg_v),
        (w_up, wu_v),
        (w_down, wd_v),
    )
    loads = [
        pltpu.make_async_copy(src, dst, load_sem.at[i]) for i, (src, dst) in enumerate(pairs)
    ]
    for load in loads:
        load.start()

    def remote(slot, src, dst, peer):
        return pltpu.make_async_remote_copy(
            src_ref=src,
            dst_ref=dst,
            send_sem=send_sem.at[slot],
            recv_sem=recv_sem.at[slot],
            device_id=peer,
            device_id_type=MESH,
        )

    pl.semaphore_wait(barrier, 6)
    first = fine.at[pl.ds(0, half)]
    fine_copies = (
        remote(0, first, ext.at[pl.ds(2 * tokens, half)], (s_prev, n)),
        remote(1, first, ext.at[pl.ds(2 * tokens + half, half)], (s_prev, n_prev)),
        remote(2, fine, ext.at[pl.ds(tokens, tokens)], (s, n_prev)),
    )
    for copy in fine_copies:
        copy.start()

    shift_row = shifts[0]
    shift_col = shifts[1]

    total = blocks * tiles
    entries = [
        lax.rem(table[0, i] - (s - 1) * blocks + total, total) for i in range(NB)
    ]

    def block_bias(j):
        hit = entries[0] == j
        for e in entries[1:]:
            hit = hit | (e == j)
        return jnp.where(hit, 0.0, HIDDEN).astype(F32)

    bias = [block_bias(j) for j in range(3 * blocks)]

    def bias_rows(values):
        row = lax.broadcasted_iota(jnp.int32, (16, tokens), 0)
        filled = jnp.zeros((16, tokens), F32)
        for b, value in enumerate(values):
            filled = jnp.where(row == b, value, filled)
        return filled.astype(BF16)

    q_send[pl.ds(0, 16), :] = bias_rows(bias[2 * blocks :])
    q_send[pl.ds(16 + width, 16), :] = bias_rows(bias[:blocks])

    for i in range(3):
        loads[i].wait()
    keys_v[...] = dot(coarse_v[...], ck_v[...]).astype(BF16)
    values_t[...] = dot(coarse_v[...], cv_v[...]).T.astype(BF16)

    for i in range(3, 8):
        loads[i].wait()
    for copy in fine_copies:
        copy.wait()

    t = lax.broadcasted_iota(jnp.int32, (tokens, 1), 0)
    row = (t >> 3) + shift_row
    col = (t & 7) + shift_col
    right = jnp.where(col >= WS, 1, 0)
    below = jnp.where(row >= rows_dev, 1, 0)
    place = (
        (row - below * rows_dev) * WS
        + (col - right * WS)
        + below * 2 * tokens
        + right * jnp.where(row >= rows_dev, half, tokens)
    )
    rolled = dot(one_hot_rows(place, 3 * tokens), ext[...])
    normed = rms_scale(rolled, gain1_v[...]).astype(BF16)
    queries = dot(normed, wq_v[...]) * (1.0 / HD**0.5)
    q_send[pl.ds(16, width), :] = queries.T.astype(BF16)
    q_copies = (
        remote(3, q_send.at[pl.ds(0, 16 + width)], q_from_prev, (s_next, n)),
        remote(4, q_send.at[pl.ds(16, 16 + width)], q_from_next, (s_prev, n)),
    )
    for copy in q_copies:
        copy.start()

    keys_fine = dot(normed, wk_v[...]).astype(BF16)
    values_fine_t = dot(normed, wv_v[...]).T.astype(BF16)

    def label(axis):
        i = lax.broadcasted_iota(jnp.int32, (tokens, tokens), axis)
        r = s * rows_dev + (i >> 3) + shift_row
        c = n * WS + (i & 7) + shift_col
        window = (i >> 6) * 4
        return (
            window
            + jnp.where(r >= rows_dev * tiles, 2, 0)
            + jnp.where(c >= WS * narrows, 1, 0)
        )

    self_bias = jnp.where(label(0) == label(1), 0.0, HIDDEN).astype(F32)
    self_bias = jnp.concatenate([self_bias, self_bias], axis=1)

    def attend(pair, q_t, biases, with_self):
        at = slice(pair * PAIR, (pair + 1) * PAIR)
        q_pair = paired(q_t)
        scores = dot(keys_v[:, at], q_pair)
        parts = [scores[b * CT : (b + 1) * CT] for b in range(blocks)]
        top = None
        for part, hide in zip(parts, biases):
            high = jnp.max(part, axis=0, keepdims=True) + hide
            top = high if top is None else jnp.maximum(top, high)
        if with_self:
            own = dot(keys_fine[:, at], q_pair) + self_bias
            top = jnp.maximum(top, jnp.max(own, axis=0, keepdims=True))
        parts = [jnp.exp(part - (top - hide)) for part, hide in zip(parts, biases)]
        amount = sum(jnp.sum(part, axis=0, keepdims=True) for part in parts)
        mixed = dot(values_t[at, :], jnp.concatenate(parts, axis=0).astype(BF16))
        if with_self:
            own = jnp.exp(own - top)
            amount = amount + jnp.sum(own, axis=0, keepdims=True)
            mixed = mixed + dot(values_fine_t[at, :], own.astype(BF16))
        return top, amount, unpaired(mixed, tokens)

    def split_heads(rows):
        halves = []
        for row in rows:
            halves += [row[:, :tokens], row[:, tokens:]]
        return jnp.concatenate(halves, axis=0)

    def neighbour(slot, q_ref, q_at, bias_at):
        loaded = q_ref[pl.ds(bias_at, 16), :].astype(F32)
        wide = jnp.concatenate([loaded, loaded], axis=1)
        biases = [wide[b : b + 1, :] for b in range(blocks)]
        tops, amounts = [], []
        for pair in range(HEADS // 2):
            q_t = q_ref[pl.ds(q_at + pair * PAIR, PAIR), :]
            top, amount, mixed = attend(pair, q_t, biases, False)
            o_send[slot, pl.ds(pair * PAIR, PAIR), :] = mixed.astype(BF16)
            tops.append(top)
            amounts.append(amount)
        st_send[slot, pl.ds(0, HEADS), :] = split_heads(tops)
        st_send[slot, pl.ds(HEADS, HEADS), :] = split_heads(amounts)

    q_copies[0].wait_recv()
    neighbour(0, q_from_prev, 16, 0)
    part_copies = [
        remote(5, st_send.at[0], st_recv.at[0], (s_prev, n)),
        remote(6, o_send.at[0], o_recv.at[0], (s_prev, n)),
    ]
    for copy in part_copies:
        copy.start()
    q_copies[1].wait_recv()
    neighbour(1, q_from_next, 0, width)
    more = [
        remote(7, st_send.at[1], st_recv.at[1], (s_next, n)),
        remote(8, o_send.at[1], o_recv.at[1], (s_next, n)),
    ]
    for copy in more:
        copy.start()
    part_copies += more

    tops, amounts = [], []
    for pair in range(HEADS // 2):
        q_t = q_send[pl.ds(16 + pair * PAIR, PAIR), :]
        top, amount, mixed = attend(pair, q_t, bias[blocks : 2 * blocks], True)
        own_o[pl.ds(pair * PAIR, PAIR), :] = mixed
        tops.append(top)
        amounts.append(amount)
    own_top, own_amount = split_heads(tops), split_heads(amounts)

    for i in range(8, len(loads)):
        loads[i].wait()
    for copy in q_copies:
        copy.wait_send()
    for copy in part_copies:
        copy.wait()

    all_tops = [own_top] + [st_recv[i, pl.ds(0, HEADS), :] for i in range(2)]
    all_amounts = [own_amount] + [st_recv[i, pl.ds(HEADS, HEADS), :] for i in range(2)]
    top = jnp.maximum(jnp.maximum(all_tops[0], all_tops[1]), all_tops[2])
    scales = [jnp.exp(x - top) for x in all_tops]
    amount = sum(a * b for a, b in zip(scales, all_amounts))
    scales = [x / amount for x in scales]
    heads = []
    for h in range(HEADS):
        at = pl.ds(h * HD, HD)
        heads.append(
            own_o[at, :] * scales[0][h : h + 1]
            + o_recv[0, at, :].astype(F32) * scales[1][h : h + 1]
            + o_recv[1, at, :].astype(F32) * scales[2][h : h + 1]
        )
    head_out = jnp.concatenate(heads, axis=0).T.astype(BF16)
    mid = rolled + dot(head_out, wo_v[...])
    normed_mid = rms_scale(mid, gain2_v[...]).astype(BF16)
    gate = dot(normed_mid, wg_v[...])
    up = dot(normed_mid, wu_v[...])
    hidden = (gate * lax.logistic(gate) * up).astype(BF16)
    block_out = mid + dot(hidden, wd_v[...])
    back[pl.ds(0, tokens), :] = block_out.astype(BF16)

    last = back.at[pl.ds(tokens - half, half)]
    back_copies = (
        remote(9, last, back.at[pl.ds(2 * tokens, half)], (s_next, n)),
        remote(10, last, back.at[pl.ds(2 * tokens + half, half)], (s_next, n_next)),
        remote(11, back.at[pl.ds(0, tokens)], back.at[pl.ds(tokens, tokens)], (s, n_next)),
    )
    for copy in back_copies:
        copy.start()
    row = (t >> 3) - shift_row
    col = (t & 7) - shift_col
    left = jnp.where(col < 0, 1, 0)
    above = jnp.where(row < 0, 1, 0)
    place = (
        (row + above * WS) * WS
        + (col + left * WS)
        + above * 2 * tokens
        + left * jnp.where(row < 0, half, tokens)
    )
    chosen = one_hot_rows(place, 3 * tokens)
    for copy in back_copies:
        copy.wait()
    out[...] = dot(chosen, back[...]).astype(BF16)


def local(
    tiles,
    narrows,
    fine,
    coarse,
    block_table,
    shifts,
    attn_gain,
    w_query,
    w_key,
    w_value,
    w_out,
    coarse_key,
    coarse_value,
    mlp_gain,
    w_gate,
    w_up,
    w_down,
):
    width = fine.shape[-1]
    tokens = fine.shape[0] * fine.shape[1]
    flat = fine.reshape(tokens, width)
    coarse_flat = coarse.reshape(-1, coarse.shape[-1])
    keys = coarse_flat.shape[0]
    gain1 = attn_gain.reshape(1, width)
    gain2 = mlp_gain.reshape(1, width)
    smem = pl.BlockSpec(memory_space=pltpu.SMEM)
    anywhere = pl.BlockSpec(memory_space=pl.ANY)

    def room(like):
        return pltpu.VMEM(like.shape, like.dtype)

    operands = (
        flat,
        coarse_flat,
        gain1,
        w_query,
        w_key,
        w_value,
        w_out,
        coarse_key,
        coarse_value,
        gain2,
        w_gate,
        w_up,
        w_down,
    )
    flops = 2 * keys * coarse.shape[-1] * 2 * width + 6 * tokens * width * w_gate.shape[-1]
    result = pl.pallas_call(
        functools.partial(kernel, tiles, narrows),
        out_shape=jax.ShapeDtypeStruct((tokens, width), fine.dtype),
        in_specs=[smem, smem] + [anywhere] * len(operands),
        out_specs=pl.BlockSpec(memory_space=pltpu.VMEM),
        scratch_shapes=[
            pltpu.VMEM((3 * tokens, width), BF16),
            pltpu.VMEM((3 * tokens, width), BF16),
        ]
        + [room(x) for x in operands[1:]]
        + [
            pltpu.VMEM((keys, width), BF16),
            pltpu.VMEM((width, keys), BF16),
            pltpu.VMEM((width + 32, tokens), BF16),
            pltpu.VMEM((width + 16, tokens), BF16),
            pltpu.VMEM((width + 16, tokens), BF16),
            pltpu.VMEM((2, width, tokens), BF16),
            pltpu.VMEM((2, 2 * HEADS, tokens), F32),
            pltpu.VMEM((2, width, tokens), BF16),
            pltpu.VMEM((2, 2 * HEADS, tokens), F32),
            pltpu.VMEM((width, tokens), F32),
            pltpu.VMEM((2 * HEADS, tokens), F32),
            pltpu.SemaphoreType.DMA((len(operands),)),
            pltpu.SemaphoreType.DMA((12,)),
            pltpu.SemaphoreType.DMA((12,)),
        ],
        compiler_params=pltpu.CompilerParams(
            collective_id=0, has_side_effects=True, vmem_limit_bytes=48 * 1024 * 1024
        ),
        cost_estimate=pl.CostEstimate(
            flops=flops, bytes_accessed=12 * 1024 * 1024, transcendentals=2 * 1024 * 1024
        ),
    )(block_table, shifts, *operands)
    return result.reshape(fine.shape)


def solution(mesh):
    placed = (
        P("tile", "narrow", None),
        P("tile", None, None),
        P("tile", None),
    ) + (P(),) * 12
    return jax.shard_map(
        functools.partial(local, mesh.shape["tile"], mesh.shape["narrow"]),
        mesh=mesh,
        in_specs=placed,
        out_specs=P("tile", "narrow", None),
        check_vma=False,
    )
```

time: 107 us -> 48.9 us (0.46)
  waiting for transfers between devices: 40.2 us -> 0 us
  Pallas kernels: 0 us -> 36.3 us
  matrix products: 19.9 us -> 0 us
  other arithmetic: 15.2 us -> 0 us
  starting transfers between devices: 10.6 us -> 0 us
  between operations: 6.86 us -> 0.02 us
  local copies, waits for them, and re-layouts: 13.5 us -> 12.1 us
    ppermute x6 -> x0, waiting for transfers between devices: 40.2 us -> none  [the longest x4 40.1 us: passed_along(): return lax.ppermute(x, axis, [(i, (i + by) % count) for i in range(count)])]
    pallas_call x0 -> x1, Pallas kernels: none -> 36.3 us  [local(): pl.pallas_call(functools.partial(kernel, tiles, narrows), out_shape=jax.S...]
    dot_general x11 -> x0, matrix products: 17.3 us -> none  [the longest x1 3.09 us: local(): mlp_sum = jnp.dot(hidden, w_down, preferred_element_type=jnp.float32)]
    ppermute x6 -> x0, starting transfers between devices: 10.6 us -> none  [the longest x1 4.06 us: with_halo(): after = lax.ppermute(initial, axis, down)]
    unnamed x25, local copies, waits for them, and re-layouts: 1.84 us -> 12.1 us
    another operation x5 -> x0, local copies, waits for them, and re-layouts: 5.76 us -> none  [the longest x4 5.55 us: to_windows(): return reordered.reshape((lead_count * across, WS * WS) + source.shape[2:])]
    concatenate x3 -> x0, other arithmetic: 3.92 us -> none  [the longest x1 3.05 us: with_halo(): x = jnp.concatenate([before, x, after], axis=dim)]
    gather x1 -> x0, local copies, waits for them, and re-layouts: 3.91 us -> none  [local(): chosen = jnp.take(nearby, local_index, axis=0).reshape(-1, CW)]
  transfers between devices with their start and end apart: 6 -> 0, of which waited for: 3 -> 0; matrix products, arithmetic and copies ran while one was open for 19% -> 0% of each run, Pallas kernels for 0% -> 0%
where the time goes in v1:
time: 48.9 us; the launch traced here: 48.4 us
  Pallas kernels  36.3 us (74%)
  local copies, waits for them, and re-layouts  12.1 us (25%)
    pallas_call x1, Pallas kernels, local(): pl.pallas_call(functools.partial(kernel, tiles, narrows), out_shape=jax.S...  36.3 us
    unnamed x25, local copies, waits for them, and re-layouts  12.1 us

profile of v1, /device:TPU:0, one launch (start us, length us, event | category | flops | bytes accessed | tf_op | source)
XLA Modules:
  0.0 48.4 jit_solution(8687241921287686335)
XLA Ops:
  0.0 0.0 copy-start
  0.0 1.2 %copy-done = bf16[4,128,1024]{2,1,0:T(8,128)(2,1)S(1)} copy-done((bf16[4,128,1024]{2,1,0:T(8,128)(2,1)S(1)}, bf16[4,128,1024]{2,1,0:T(8,128)(2,1)}, u32[]{:S(2)}) %copy-start) | copy-done | bytes 1048600
  1.2 0.0 copy-start.1
  1.2 1.2 %copy-done.1 = bf16[1024,512]{1,0:T(8,128)(2,1)S(1)} copy-done((bf16[1024,512]{1,0:T(8,128)(2,1)S(1)}, bf16[1024,512]{1,0:T(8,128)(2,1)}, u32[]{:S(2)}) %copy-start.1) | copy-done | bytes 1048600
  2.5 0.0 copy-start.2
  2.5 1.2 %copy-done.2 = bf16[1024,512]{1,0:T(8,128)(2,1)S(1)} copy-done((bf16[1024,512]{1,0:T(8,128)(2,1)S(1)}, bf16[1024,512]{1,0:T(8,128)(2,1)}, u32[]{:S(2)}) %copy-start.2) | copy-done | bytes 1048600
  3.7 0.0 copy-start.3
  3.7 1.0 %copy-done.3 = bf16[512,512]{1,0:T(8,128)(2,1)S(1)} copy-done((bf16[512,512]{1,0:T(8,128)(2,1)S(1)}, bf16[512,512]{1,0:T(8,128)(2,1)}, u32[]{:S(2)}) %copy-start.3) | copy-done | bytes 524312
  4.7 0.0 copy-start.4
  4.7 1.0 %copy-done.4 = bf16[512,512]{1,0:T(8,128)(2,1)S(1)} copy-done((bf16[512,512]{1,0:T(8,128)(2,1)S(1)}, bf16[512,512]{1,0:T(8,128)(2,1)}, u32[]{:S(2)}) %copy-start.4) | copy-done | bytes 524312
  5.8 0.0 copy-start.5
  5.8 1.0 %copy-done.5 = bf16[512,512]{1,0:T(8,128)(2,1)S(1)} copy-done((bf16[512,512]{1,0:T(8,128)(2,1)S(1)}, bf16[512,512]{1,0:T(8,128)(2,1)}, u32[]{:S(2)}) %copy-start.5) | copy-done | bytes 524312
  6.8 0.0 copy-start.6
  6.8 1.0 %copy-done.6 = bf16[512,512]{1,0:T(8,128)(2,1)S(1)} copy-done((bf16[512,512]{1,0:T(8,128)(2,1)S(1)}, bf16[512,512]{1,0:T(8,128)(2,1)}, u32[]{:S(2)}) %copy-start.6) | copy-done | bytes 524312
  7.8 0.0 copy-start.7
  7.8 0.9 %copy-done.7 = bf16[16,8,512]{2,1,0:T(8,128)(2,1)S(1)} copy-done((bf16[16,8,512]{2,1,0:T(8,128)(2,1)S(1)}, bf16[16,8,512]{2,1,0:T(8,128)(2,1)}, u32[]{:S(2)}) %copy-start.7) | copy-done | bytes 131096
  8.7 0.0 copy-start.8
  8.8 0.7 %copy-done.8 = f32[512]{0:T(512)S(1)} copy-done((f32[512]{0:T(512)S(1)}, f32[512]{0:T(512)}, u32[]{:S(2)}) %copy-start.8) | copy-done | bytes 2072
  9.4 0.0 copy-start.9
  9.4 0.7 %copy-done.9 = f32[512]{0:T(512)S(1)} copy-done((f32[512]{0:T(512)S(1)}, f32[512]{0:T(512)}, u32[]{:S(2)}) %copy-start.9) | copy-done | bytes 2072
  10.1 0.0 copy-start.10
  10.1 0.7 %copy-done.10 = s32[1,8]{1,0:T(1,128)S(1)} copy-done((s32[1,8]{1,0:T(1,128)S(1)}, s32[1,8]{1,0:T(1,128)}, u32[]{:S(2)}) %copy-start.10) | copy-done | bytes 56
  10.8 0.0 copy-start.11
  10.8 0.7 %copy-done.11 = s32[2]{0:T(128)S(1)} copy-done((s32[2]{0:T(128)S(1)}, s32[2]{0:T(128)}, u32[]{:S(2)}) %copy-start.11) | copy-done | bytes 32
  11.4 36.3 %shard_map.145 = bf16[128,512]{1,0:T(8,128)(2,1)S(1)} custom-call(s32[1,8]{1,0:T(1,128)S(1)} %copy-done.10, s32[2]{0:T(128)S(1)} %copy-done.11, bf16[128,512]{1,0:T(8,128)(2,1)S(1)} %bitcast.7, bf16[512,1024]{1,0:T(8,128)(2,1)S(1)} %bitcast.5, f32[1,512]{1,0:T(1,128)S(1)} %bitcast.8, bf16[512,512]{1,0:T(8,128)(2,1)S(1)} %copy-done.3, ...), custom_call_target="tpu_custom_call" | custom-call | flops 1879048192 | bytes 12582912 | tf_op jit(solution)/shard_map/pallas_call | solution.py:401
  47.7 0.7 %copy.17 = bf16[16,8,512]{2,1,0:T(8,128)(2,1)} copy(bf16[16,8,512]{2,1,0:T(8,128)(2,1)S(1)} %bitcast.6) | data formatting | bytes 262144
Async XLA Ops:
  0.0 1.2 %copy-start = (bf16[4,128,1024]{2,1,0:T(8,128)(2,1)S(1)}, bf16[4,128,1024]{2,1,0:T(8,128)(2,1)}, u32[]{:S(2)}) copy-start(bf16[4,128,1024]{2,1,0:T(8,128)(2,1)} %param.16) | copy-start | bytes 3145732
  1.2 1.2 %copy-start.1 = (bf16[1024,512]{1,0:T(8,128)(2,1)S(1)}, bf16[1024,512]{1,0:T(8,128)(2,1)}, u32[]{:S(2)}) copy-start(bf16[1024,512]{1,0:T(8,128)(2,1)} %coarse_key.1) | copy-start | bytes 3145732
  2.5 1.2 %copy-start.2 = (bf16[1024,512]{1,0:T(8,128)(2,1)S(1)}, bf16[1024,512]{1,0:T(8,128)(2,1)}, u32[]{:S(2)}) copy-start(bf16[1024,512]{1,0:T(8,128)(2,1)} %coarse_value.1) | copy-start | bytes 3145732
  3.7 1.0 %copy-start.3 = (bf16[512,512]{1,0:T(8,128)(2,1)S(1)}, bf16[512,512]{1,0:T(8,128)(2,1)}, u32[]{:S(2)}) copy-start(bf16[512,512]{1,0:T(8,128)(2,1)} %w_query.1) | copy-start | bytes 1572868
  4.7 1.0 %copy-start.4 = (bf16[512,512]{1,0:T(8,128)(2,1)S(1)}, bf16[512,512]{1,0:T(8,128)(2,1)}, u32[]{:S(2)}) copy-start(bf16[512,512]{1,0:T(8,128)(2,1)} %w_key.1) | copy-start | bytes 1572868
  5.8 1.0 %copy-start.5 = (bf16[512,512]{1,0:T(8,128)(2,1)S(1)}, bf16[512,512]{1,0:T(8,128)(2,1)}, u32[]{:S(2)}) copy-start(bf16[512,512]{1,0:T(8,128)(2,1)} %w_value.1) | copy-start | bytes 1572868
  6.8 1.0 %copy-start.6 = (bf16[512,512]{1,0:T(8,128)(2,1)S(1)}, bf16[512,512]{1,0:T(8,128)(2,1)}, u32[]{:S(2)}) copy-start(bf16[512,512]{1,0:T(8,128)(2,1)} %w_out.1) | copy-start | bytes 1572868
  7.8 0.9 %copy-start.7 = (bf16[16,8,512]{2,1,0:T(8,128)(2,1)S(1)}, bf16[16,8,512]{2,1,0:T(8,128)(2,1)}, u32[]{:S(2)}) copy-start(bf16[16,8,512]{2,1,0:T(8,128)(2,1)} %param.15) | copy-start | bytes 393220
  8.7 0.7 %copy-start.8 = (f32[512]{0:T(512)S(1)}, f32[512]{0:T(512)}, u32[]{:S(2)}) copy-start(f32[512]{0:T(512)} %param.19) | copy-start | bytes 6148
  9.4 0.7 %copy-start.9 = (f32[512]{0:T(512)S(1)}, f32[512]{0:T(512)}, u32[]{:S(2)}) copy-start(f32[512]{0:T(512)} %param.26) | copy-start | bytes 6148
  10.1 0.7 %copy-start.10 = (s32[1,8]{1,0:T(1,128)S(1)}, s32[1,8]{1,0:T(1,128)}, u32[]{:S(2)}) copy-start(s32[1,8]{1,0:T(1,128)} %table.1) | copy-start | bytes 100
  10.8 0.7 %copy-start.11 = (s32[2]{0:T(128)S(1)}, s32[2]{0:T(128)}, u32[]{:S(2)}) copy-start(s32[2]{0:T(128)} %shifts.1) | copy-start | bytes 28

commit v2 on v1

v2 whole, which is shorter than its diff:
```python
import functools

import jax
import jax.numpy as jnp
from jax import lax
from jax.experimental import pallas as pl
from jax.experimental.pallas import tpu as pltpu
from jax.sharding import PartitionSpec as P

WS = 8
HD = 64
HEADS = 8
PAIR = 2 * HD
CT = 128
NB = 8
HIDDEN = -1e30
UNSEEN = -1e29
MESH = pl.DeviceIdType.MESH
F32 = jnp.float32
BF16 = jnp.bfloat16


def dot(a, b):
    return jnp.dot(a, b, preferred_element_type=F32)


def rms_scale(values, gain_vec):
    mean_square = jnp.mean(values * values, axis=-1, keepdims=True)
    return values * lax.rsqrt(mean_square + 1e-06) * gain_vec


def one_hot_rows(index, count):
    lanes = lax.broadcasted_iota(jnp.int32, (index.shape[0], count), 1)
    return (lanes == index).astype(F32).astype(BF16)


def paired(q_t):
    zero = jnp.zeros((HD, q_t.shape[1]), q_t.dtype)
    upper = jnp.concatenate([q_t[:HD], zero], axis=1)
    lower = jnp.concatenate([zero, q_t[HD:]], axis=1)
    return jnp.concatenate([upper, lower], axis=0)


def unpaired(both, tokens):
    return jnp.concatenate([both[:HD, :tokens], both[HD:, tokens:]], axis=0)


def kernel(
    tiles,
    narrows,
    table,
    shifts,
    fine,
    coarse,
    attn_gain,
    w_query,
    w_key,
    w_value,
    w_out,
    coarse_key,
    coarse_value,
    mlp_gain,
    w_gate,
    w_up,
    w_down,
    out,
    ext,
    far,
    coarse_v,
    gain1_v,
    wq_v,
    wk_v,
    wv_v,
    wo_v,
    ck_v,
    cv_v,
    gain2_v,
    wg_v,
    wu_v,
    wd_v,
    keys_v,
    values_t,
    table_send,
    table_recv,
    o_send,
    st_send,
    o_recv,
    st_recv,
    own_o,
    load_sem,
    send_sem,
    recv_sem,
):
    s = lax.axis_index("tile")
    n = lax.axis_index("narrow")
    s_next, s_prev = lax.rem(s + 1, tiles), lax.rem(s + tiles - 1, tiles)
    s_next2, s_prev2 = lax.rem(s + 2, tiles), lax.rem(s + tiles - 2, tiles)
    n_next, n_prev = lax.rem(n + 1, narrows), lax.rem(n + narrows - 1, narrows)
    tokens, width = fine.shape
    half = WS * WS
    rows_dev = tokens // WS
    blocks = coarse.shape[0] // CT
    two_sides = narrows > 2

    barrier = pltpu.get_barrier_semaphore()
    for peer in (
        (s_next, n),
        (s_prev, n),
        (s_next2, n),
        (s_prev2, n),
        (s, n_next),
        (s, n_prev),
    ):
        pl.semaphore_signal(barrier, inc=1, device_id=peer, device_id_type=MESH)

    pairs = (
        (coarse, coarse_v),
        (coarse_key, ck_v),
        (coarse_value, cv_v),
        (fine, ext.at[pl.ds(0, tokens)]),
        (attn_gain, gain1_v),
        (w_query, wq_v),
        (w_key, wk_v),
        (w_value, wv_v),
        (w_out, wo_v),
        (mlp_gain, gain2_v),
        (w_gate, wg_v),
        (w_up, wu_v),
        (w_down, wd_v),
    )
    loads = [
        pltpu.make_async_copy(src, dst, load_sem.at[i]) for i, (src, dst) in enumerate(pairs)
    ]
    for load in loads:
        load.start()

    def remote(slot, src, dst, peer):
        return pltpu.make_async_remote_copy(
            src_ref=src,
            dst_ref=dst,
            send_sem=send_sem.at[slot],
            recv_sem=recv_sem.at[slot],
            device_id=peer,
            device_id_type=MESH,
        )

    total = blocks * tiles
    entries = [
        lax.rem(table[0, i] - (s - 1) * blocks + total, total) for i in range(NB)
    ]

    def block_bias(j):
        hit = entries[0] == j
        for e in entries[1:]:
            hit = hit | (e == j)
        return jnp.where(hit, 0.0, HIDDEN).astype(F32)

    bias = [block_bias(j) for j in range(3 * blocks)]
    row = lax.broadcasted_iota(jnp.int32, (16, tokens), 0)
    filled = jnp.zeros((16, tokens), F32)
    for b in range(blocks):
        filled = jnp.where(row == b, bias[2 * blocks + b], filled)
        filled = jnp.where(row == 8 + b, bias[b], filled)
    table_send[...] = filled

    above, below, side, other = tokens, 2 * tokens, 3 * tokens, 5 * tokens
    pl.semaphore_wait(barrier, 6)
    table_copies = (
        remote(0, table_send.at[pl.ds(0, 8)], table_recv.at[0], (s_next, n)),
        remote(1, table_send.at[pl.ds(8, 8)], table_recv.at[1], (s_prev, n)),
    )
    to_prev = remote(2, fine, ext.at[pl.ds(below, tokens)], (s_prev, n))
    to_next = remote(3, fine, ext.at[pl.ds(above, tokens)], (s_next, n))
    to_far = remote(4, fine.at[pl.ds(0, half)], far, (s_prev2, n))
    sides = [remote(5, fine, ext.at[pl.ds(side, tokens)], (s, n_prev))]
    if two_sides:
        sides.append(remote(6, fine, ext.at[pl.ds(other, tokens)], (s, n_next)))
    for copy in (*table_copies, to_prev, to_next, to_far, *sides):
        copy.start()

    shift_row = shifts[0]
    shift_col = shifts[1]

    for i in range(3):
        loads[i].wait()
    keys_v[...] = dot(coarse_v[...], ck_v[...]).astype(BF16)
    values_t[...] = dot(coarse_v[...], cv_v[...]).T.astype(BF16)

    for i in range(3, 8):
        loads[i].wait()

    def normed_of(raw):
        return rms_scale(raw.astype(F32), gain1_v[...]).astype(BF16)

    def queries_of(raw):
        queries = dot(normed_of(raw), wq_v[...]) * (1.0 / HD**0.5)
        return queries.T.astype(BF16)

    for copy in table_copies:
        copy.wait()
    early = (lax.broadcasted_iota(jnp.int32, (1, tokens), 1) >> 3) < shift_row

    def token_bias(upper, lower):
        rows = []
        for x, y in zip(upper, lower):
            one = jnp.where(early, x, y)
            rows.append(jnp.concatenate([one, one], axis=1))
        return rows

    by_prev = [table_recv[0, pl.ds(b, 1), :] for b in range(blocks)]
    by_own = bias[blocks : 2 * blocks]
    by_next = [table_recv[1, pl.ds(b, 1), :] for b in range(blocks)]
    by_none = [HIDDEN] * blocks

    def attend(pair, q_t, biases):
        at = slice(pair * PAIR, (pair + 1) * PAIR)
        scores = dot(keys_v[:, at], paired(q_t[at]))
        parts = [scores[b * CT : (b + 1) * CT] for b in range(blocks)]
        top = None
        for part, hide in zip(parts, biases):
            high = jnp.max(part, axis=0, keepdims=True) + hide
            top = high if top is None else jnp.maximum(top, high)
        unseen = top < UNSEEN
        parts = [
            jnp.exp(part - jnp.where(unseen, -HIDDEN, top - hide))
            for part, hide in zip(parts, biases)
        ]
        amount = sum(jnp.sum(part, axis=0, keepdims=True) for part in parts)
        mixed = dot(values_t[at, :], jnp.concatenate(parts, axis=0).astype(BF16))
        return top, amount, unpaired(mixed, tokens)

    def split_heads(rows):
        halves = []
        for row in rows:
            halves += [row[:, :tokens], row[:, tokens:]]
        return jnp.concatenate(halves, axis=0)

    def cross(q_t, biases, store):
        tops, amounts = [], []
        for pair in range(HEADS // 2):
            top, amount, mixed = attend(pair, q_t, biases)
            store(pair, mixed)
            tops.append(top)
            amounts.append(amount)
        return split_heads(tops), split_heads(amounts)

    def neighbour(slot, raw, biases, peer):
        def store(pair, mixed):
            o_send[slot, pl.ds(pair * PAIR, PAIR), :] = mixed.astype(BF16)

        top, amount = cross(queries_of(raw), biases, store)
        st_send[slot, pl.ds(0, HEADS), :] = top
        st_send[slot, pl.ds(HEADS, HEADS), :] = amount
        copies = [
            remote(7 + 2 * slot, st_send.at[slot], st_recv.at[slot], peer),
            remote(8 + 2 * slot, o_send.at[slot], o_recv.at[slot], peer),
        ]
        for copy in copies:
            copy.start()
        return copies

    def keep(pair, mixed):
        own_o[0, pl.ds(pair * PAIR, PAIR), :] = mixed

    own = ext[pl.ds(0, tokens), :]
    own_q = queries_of(own)
    own_top, own_amount = cross(own_q, token_bias(by_prev, by_own), keep)

    forwards = []

    def forward(slot, at, place):
        src = ext.at[pl.ds(at, half)]
        copies = [remote(slot, src, ext.at[pl.ds(side + place, half)], (s, n_prev))]
        if two_sides:
            copies.append(
                remote(slot + 1, src, ext.at[pl.ds(other + place, half)], (s, n_next))
            )
        for copy in copies:
            copy.start()
        return copies

    to_prev.wait_recv()
    forwards += forward(13, below, tokens + half)
    part_copies = neighbour(
        0, ext[pl.ds(below, tokens), :], token_bias(by_own, by_next), (s_next, n)
    )
    to_next.wait_recv()
    forwards += forward(15, above + tokens - half, tokens)
    part_copies += neighbour(
        1, ext[pl.ds(above, tokens), :], token_bias(by_none, by_prev), (s_prev, n)
    )
    to_far.wait_recv()
    far_raw = far[...]
    part_copies += neighbour(
        2,
        jnp.concatenate([far_raw, far_raw], axis=0),
        token_bias(by_next, by_none),
        (s_next2, n),
    )

    for copy in sides:
        copy.wait_recv()
    for copy in forwards:
        copy.wait_recv()
    near = 6 * half
    k = lax.broadcasted_iota(jnp.int32, (near, 1), 0)
    row = (k >> 4) + shift_row - WS
    col = (k & 15) + shift_col - WS
    is_above, is_below = row < 0, row >= rows_dev
    is_left, is_right = col < 0, col >= WS
    row_in = jnp.where(is_above, row + rows_dev, jnp.where(is_below, row - rows_dev, row))
    col_in = jnp.where(is_left, col + WS, jnp.where(is_right, col - WS, col))
    middle = jnp.where(is_above, above, jnp.where(is_below, below, 0))
    beside = jnp.where(
        is_above, tokens - half, jnp.where(is_below, tokens + half, 0)
    ) + jnp.where(is_left, other if two_sides else side, side)
    place = jnp.where(is_left | is_right, beside, middle) + row_in * WS + col_in
    around = dot(one_hot_rows(place, ext.shape[0]), ext[...])
    normed = normed_of(around)
    keys_fine = dot(normed, wk_v[...]).astype(BF16)
    values_fine_t = dot(normed, wv_v[...]).T.astype(BF16)

    def label(row, col):
        g = s * rows_dev + row
        g = jnp.where(g < 0, g + rows_dev * tiles, g)
        g = jnp.where(g >= rows_dev * tiles, g - rows_dev * tiles, g)
        h = n * WS + col
        h = jnp.where(h < 0, h + WS * narrows, h)
        h = jnp.where(h >= WS * narrows, h - WS * narrows, h)
        window = ((row - shift_row + WS) >> 3) * 2 + ((col - shift_col + WS) >> 3)
        return window * 4 + jnp.where(g < shift_row, 2, 0) + jnp.where(h < shift_col, 1, 0)

    k = lax.broadcasted_iota(jnp.int32, (near, tokens), 0)
    t = lax.broadcasted_iota(jnp.int32, (near, tokens), 1)
    same = label((k >> 4) + shift_row - WS, (k & 15) + shift_col - WS) == label(t >> 3, t & 7)
    hide = jnp.where(same, 0.0, HIDDEN).astype(F32)
    hide = jnp.concatenate([hide, hide], axis=1)
    tops, amounts = [], []
    for pair in range(HEADS // 2):
        at = slice(pair * PAIR, (pair + 1) * PAIR)
        scores = dot(keys_fine[:, at], paired(own_q[at])) + hide
        top = jnp.max(scores, axis=0, keepdims=True)
        weights = jnp.exp(scores - top)
        tops.append(top)
        amounts.append(jnp.sum(weights, axis=0, keepdims=True))
        mixed = dot(values_fine_t[at, :], weights.astype(BF16))
        own_o[1, pl.ds(pair * PAIR, PAIR), :] = unpaired(mixed, tokens)
    self_top, self_amount = split_heads(tops), split_heads(amounts)

    for i in range(8, len(loads)):
        loads[i].wait()
    for copy in part_copies:
        copy.wait()
    for copy in (to_prev, to_next, to_far, *sides, *forwards):
        copy.wait_send()

    all_tops = [own_top, self_top] + [st_recv[i, pl.ds(0, HEADS), :] for i in range(3)]
    all_amounts = [own_amount, self_amount] + [
        st_recv[i, pl.ds(HEADS, HEADS), :] for i in range(3)
    ]
    top = functools.reduce(jnp.maximum, all_tops)
    scales = [jnp.exp(x - top) for x in all_tops]
    amount = sum(a * b for a, b in zip(scales, all_amounts))
    scales = [x / amount for x in scales]
    heads = []
    for h in range(HEADS):
        at = pl.ds(h * HD, HD)
        mixed = own_o[0, at, :] * scales[0][h : h + 1] + own_o[1, at, :] * scales[1][h : h + 1]
        for i in range(3):
            mixed = mixed + o_recv[i, at, :].astype(F32) * scales[2 + i][h : h + 1]
        heads.append(mixed)
    head_out = jnp.concatenate(heads, axis=0).T.astype(BF16)
    mid = ext[pl.ds(0, tokens), :].astype(F32) + dot(head_out, wo_v[...])
    normed_mid = rms_scale(mid, gain2_v[...]).astype(BF16)
    gate = dot(normed_mid, wg_v[...])
    up = dot(normed_mid, wu_v[...])
    hidden = (gate * lax.logistic(gate) * up).astype(BF16)
    out[...] = (mid + dot(hidden, wd_v[...])).astype(BF16)


def local(
    tiles,
    narrows,
    fine,
    coarse,
    block_table,
    shifts,
    attn_gain,
    w_query,
    w_key,
    w_value,
    w_out,
    coarse_key,
    coarse_value,
    mlp_gain,
    w_gate,
    w_up,
    w_down,
):
    width = fine.shape[-1]
    tokens = fine.shape[0] * fine.shape[1]
    flat = fine.reshape(tokens, width)
    coarse_flat = coarse.reshape(-1, coarse.shape[-1])
    keys = coarse_flat.shape[0]
    gain1 = attn_gain.reshape(1, width)
    gain2 = mlp_gain.reshape(1, width)
    smem = pl.BlockSpec(memory_space=pltpu.SMEM)
    anywhere = pl.BlockSpec(memory_space=pltpu.HBM)

    def room(like):
        return pltpu.VMEM(like.shape, like.dtype)

    operands = (
        flat,
        coarse_flat,
        gain1,
        w_query,
        w_key,
        w_value,
        w_out,
        coarse_key,
        coarse_value,
        gain2,
        w_gate,
        w_up,
        w_down,
    )
    flops = 2 * keys * coarse.shape[-1] * 2 * width + 6 * tokens * width * w_gate.shape[-1]
    result = pl.pallas_call(
        functools.partial(kernel, tiles, narrows),
        out_shape=jax.ShapeDtypeStruct((tokens, width), fine.dtype),
        in_specs=[smem, smem] + [anywhere] * len(operands),
        out_specs=pl.BlockSpec(memory_space=pltpu.VMEM),
        scratch_shapes=[
            pltpu.VMEM(((7 if narrows > 2 else 5) * tokens, width), BF16),
            pltpu.VMEM((WS * WS, width), BF16),
        ]
        + [room(x) for x in operands[1:]]
        + [
            pltpu.VMEM((keys, width), BF16),
            pltpu.VMEM((width, keys), BF16),
            pltpu.VMEM((16, tokens), F32),
            pltpu.VMEM((2, 8, tokens), F32),
            pltpu.VMEM((3, width, tokens), BF16),
            pltpu.VMEM((3, 2 * HEADS, tokens), F32),
            pltpu.VMEM((3, width, tokens), BF16),
            pltpu.VMEM((3, 2 * HEADS, tokens), F32),
            pltpu.VMEM((2, width, tokens), F32),
            pltpu.SemaphoreType.DMA((len(operands),)),
            pltpu.SemaphoreType.DMA((17,)),
            pltpu.SemaphoreType.DMA((17,)),
        ],
        compiler_params=pltpu.CompilerParams(
            collective_id=0, has_side_effects=True, vmem_limit_bytes=60 * 1024 * 1024
        ),
        cost_estimate=pl.CostEstimate(
            flops=flops, bytes_accessed=12 * 1024 * 1024, transcendentals=2 * 1024 * 1024
        ),
    )(block_table, shifts, *operands)
    return result.reshape(fine.shape)


def solution(mesh):
    placed = (
        P("tile", "narrow", None),
        P("tile", None, None),
        P("tile", None),
    ) + (P(),) * 12
    return jax.shard_map(
        functools.partial(local, mesh.shape["tile"], mesh.shape["narrow"]),
        mesh=mesh,
        in_specs=placed,
        out_specs=P("tile", "narrow", None),
        check_vma=False,
    )
```

time: 48.9 us -> 30 us (0.61)
  local copies, waits for them, and re-layouts: 12.1 us -> 1.57 us
  Pallas kernels: 36.3 us -> 28.3 us
    unnamed x25 -> x1, local copies, waits for them, and re-layouts: 12.1 us -> 1.57 us
    pallas_call x1, Pallas kernels: 36.3 us -> 28.3 us  [local(): pl.pallas_call(functools.partial(kernel, tiles, narrows), out_shape=jax.S...]
where the time goes in v2:
time: 30 us; the launch traced here: 29.9 us
  Pallas kernels  28.3 us (94%)
  local copies, waits for them, and re-layouts  1.57 us (5%)
    pallas_call x1, Pallas kernels, local(): pl.pallas_call(functools.partial(kernel, tiles, narrows), out_shape=jax.S...  28.3 us
    unnamed x1, local copies, waits for them, and re-layouts  1.57 us

profile of v2, /device:TPU:0, one launch (start us, length us, event | category | flops | bytes accessed | tf_op | source)
XLA Modules:
  0.0 29.9 jit_solution(7521508395626616314)
XLA Ops:
  0.0 28.3 %shard_map.145 = bf16[128,512]{1,0:T(8,128)(2,1)} custom-call(s32[1,8]{1,0:T(1,128)} %table.1, s32[2]{0:T(128)} %shifts.1, bf16[128,512]{1,0:T(8,128)(2,1)} %bitcast.7, bf16[512,1024]{1,0:T(8,128)(2,1)} %bitcast.5, f32[1,512]{1,0:T(1,128)} %bitcast.8, bf16[512,512]{1,0:T(8,128)(2,1)} %w_query.1, bf16[512,512]{1,0:T(8,128)(2,1)} %w_key.1, ...), custom_call_target="tpu_custom_call" | custom-call | flops 1879048192 | bytes 12582912 | tf_op jit(solution)/shard_map/pallas_call | solution.py:429
  28.3 1.6 %copy.17 = bf16[16,8,512]{2,1,0:T(8,128)(2,1)} copy(bf16[16,8,512]{2,1,0:T(8,128)(2,1)} %bitcast.6) | data formatting | bytes 262144

commit v3 on v2

--- a/solution.py
+++ b/solution.py
@@ -175,7 +175,7 @@
     sides = [remote(5, fine, ext.at[pl.ds(side, tokens)], (s, n_prev))]
     if two_sides:
         sides.append(remote(6, fine, ext.at[pl.ds(other, tokens)], (s, n_next)))
-    for copy in (*table_copies, to_prev, to_next, to_far, *sides):
+    for copy in (*table_copies, to_far, to_prev, *sides):
         copy.start()
 
     shift_row = shifts[0]
@@ -184,6 +184,8 @@
     for i in range(3):
         loads[i].wait()
     keys_v[...] = dot(coarse_v[...], ck_v[...]).astype(BF16)
+    to_prev.wait_send()
+    to_next.start()
     values_t[...] = dot(coarse_v[...], cv_v[...]).T.astype(BF16)
 
     for i in range(3, 8):
@@ -262,10 +264,6 @@
     def keep(pair, mixed):
         own_o[0, pl.ds(pair * PAIR, PAIR), :] = mixed
 
-    own = ext[pl.ds(0, tokens), :]
-    own_q = queries_of(own)
-    own_top, own_amount = cross(own_q, token_bias(by_prev, by_own), keep)
-
     forwards = []
 
     def forward(slot, at, place):
@@ -279,9 +277,17 @@
             copy.start()
         return copies
 
+    to_far.wait_recv()
+    far_raw = far[...]
+    part_copies = neighbour(
+        2,
+        jnp.concatenate([far_raw, far_raw], axis=0),
+        token_bias(by_next, by_none),
+        (s_next2, n),
+    )
     to_prev.wait_recv()
     forwards += forward(13, below, tokens + half)
-    part_copies = neighbour(
+    part_copies += neighbour(
         0, ext[pl.ds(below, tokens), :], token_bias(by_own, by_next), (s_next, n)
     )
     to_next.wait_recv()
@@ -289,14 +295,9 @@
     part_copies += neighbour(
         1, ext[pl.ds(above, tokens), :], token_bias(by_none, by_prev), (s_prev, n)
     )
-    to_far.wait_recv()
-    far_raw = far[...]
-    part_copies += neighbour(
-        2,
-        jnp.concatenate([far_raw, far_raw], axis=0),
-        token_bias(by_next, by_none),
-        (s_next2, n),
-    )
+
+    own_q = queries_of(ext[pl.ds(0, tokens), :])
+    own_top, own_amount = cross(own_q, token_bias(by_prev, by_own), keep)
 
     for copy in sides:
         copy.wait_recv()
@@ -351,7 +352,7 @@
         loads[i].wait()
     for copy in part_copies:
         copy.wait()
-    for copy in (to_prev, to_next, to_far, *sides, *forwards):
+    for copy in (to_next, to_far, *sides, *forwards):
         copy.wait_send()
 
     all_tops = [own_top, self_top] + [st_recv[i, pl.ds(0, HEADS), :] for i in range(3)]

time: 30 us -> 28.5 us (0.950)
  Pallas kernels: 28.3 us -> 26.8 us
    pallas_call x1, Pallas kernels: 28.3 us -> 26.8 us  [local(): pl.pallas_call(functools.partial(kernel, tiles, narrows), out_shape=jax.S...]
where the time goes in v3:
time: 28.5 us; the launch traced here: 28.4 us
  Pallas kernels  26.8 us (94%)
  local copies, waits for them, and re-layouts  1.57 us (6%)
    pallas_call x1, Pallas kernels, local(): pl.pallas_call(functools.partial(kernel, tiles, narrows), out_shape=jax.S...  26.8 us
    unnamed x1, local copies, waits for them, and re-layouts  1.57 us

profile of v3, /device:TPU:0, one launch (start us, length us, event | category | flops | bytes accessed | tf_op | source)
XLA Modules:
  0.0 28.4 jit_solution(4974521180365361745)
XLA Ops:
  0.0 26.8 %shard_map.145 = bf16[128,512]{1,0:T(8,128)(2,1)} custom-call(s32[1,8]{1,0:T(1,128)} %table.1, s32[2]{0:T(128)} %shifts.1, bf16[128,512]{1,0:T(8,128)(2,1)} %bitcast.7, bf16[512,1024]{1,0:T(8,128)(2,1)} %bitcast.5, f32[1,512]{1,0:T(1,128)} %bitcast.8, bf16[512,512]{1,0:T(8,128)(2,1)} %w_query.1, bf16[512,512]{1,0:T(8,128)(2,1)} %w_key.1, ...), custom_call_target="tpu_custom_call" | custom-call | flops 1879048192 | bytes 12582912 | tf_op jit(solution)/shard_map/pallas_call | solution.py:430
  26.8 1.6 %copy.17 = bf16[16,8,512]{2,1,0:T(8,128)(2,1)} copy(bf16[16,8,512]{2,1,0:T(8,128)(2,1)} %bitcast.6) | data formatting | bytes 262144

commit v4 on v3

--- a/solution.py
+++ b/solution.py
@@ -48,8 +48,8 @@
 def kernel(
     tiles,
     narrows,
-    table,
-    shifts,
+    table_in,
+    shifts_in,
     fine,
     coarse,
     attn_gain,
@@ -87,6 +87,8 @@
     o_recv,
     st_recv,
     own_o,
+    table,
+    shifts,
     load_sem,
     send_sem,
     recv_sem,
@@ -117,6 +119,8 @@
         (coarse, coarse_v),
         (coarse_key, ck_v),
         (coarse_value, cv_v),
+        (table_in, table),
+        (shifts_in, shifts),
         (fine, ext.at[pl.ds(0, tokens)]),
         (attn_gain, gain1_v),
         (w_query, wq_v),
@@ -131,8 +135,8 @@
     loads = [
         pltpu.make_async_copy(src, dst, load_sem.at[i]) for i, (src, dst) in enumerate(pairs)
     ]
-    for load in loads:
-        load.start()
+    for i in (*range(3, 5), *range(3), *range(5, 8)):
+        loads[i].start()
 
     def remote(slot, src, dst, peer):
         return pltpu.make_async_remote_copy(
@@ -144,10 +148,27 @@
             device_id_type=MESH,
         )
 
+    above, below, side, other = tokens, 2 * tokens, 3 * tokens, 5 * tokens
+    pl.semaphore_wait(barrier, 6)
+    to_prev = remote(2, fine, ext.at[pl.ds(below, tokens)], (s_prev, n))
+    to_next = remote(3, fine, ext.at[pl.ds(above, tokens)], (s_next, n))
+    to_far = remote(4, fine.at[pl.ds(0, half)], far, (s_prev2, n))
+    sides = [remote(5, fine, ext.at[pl.ds(side, tokens)], (s, n_prev))]
+    if two_sides:
+        sides.append(remote(6, fine, ext.at[pl.ds(other, tokens)], (s, n_next)))
+    for copy in (to_far, to_prev, *sides):
+        copy.start()
+    for i in range(8, len(loads)):
+        loads[i].start()
+
+    loads[3].wait()
+    loads[4].wait()
     total = blocks * tiles
-    entries = [
-        lax.rem(table[0, i] - (s - 1) * blocks + total, total) for i in range(NB)
-    ]
+    entries = []
+    for i in range(NB):
+        e = table[0, i] - (s - 1) * blocks
+        e = jnp.where(e < 0, e + total, e)
+        entries.append(jnp.where(e >= total, e - total, e))
 
     def block_bias(j):
         hit = entries[0] == j
@@ -163,32 +184,22 @@
         filled = jnp.where(row == 8 + b, bias[b], filled)
     table_send[...] = filled
 
-    above, below, side, other = tokens, 2 * tokens, 3 * tokens, 5 * tokens
-    pl.semaphore_wait(barrier, 6)
     table_copies = (
         remote(0, table_send.at[pl.ds(0, 8)], table_recv.at[0], (s_next, n)),
         remote(1, table_send.at[pl.ds(8, 8)], table_recv.at[1], (s_prev, n)),
     )
-    to_prev = remote(2, fine, ext.at[pl.ds(below, tokens)], (s_prev, n))
-    to_next = remote(3, fine, ext.at[pl.ds(above, tokens)], (s_next, n))
-    to_far = remote(4, fine.at[pl.ds(0, half)], far, (s_prev2, n))
-    sides = [remote(5, fine, ext.at[pl.ds(side, tokens)], (s, n_prev))]
-    if two_sides:
-        sides.append(remote(6, fine, ext.at[pl.ds(other, tokens)], (s, n_next)))
-    for copy in (*table_copies, to_far, to_prev, *sides):
+    for copy in table_copies:
         copy.start()
-
     shift_row = shifts[0]
     shift_col = shifts[1]
 
     for i in range(3):
         loads[i].wait()
     keys_v[...] = dot(coarse_v[...], ck_v[...]).astype(BF16)
-    to_prev.wait_send()
+    values_t[...] = dot(coarse_v[...], cv_v[...]).T.astype(BF16)
     to_next.start()
-    values_t[...] = dot(coarse_v[...], cv_v[...]).T.astype(BF16)
-
-    for i in range(3, 8):
+
+    for i in range(5, 10):
         loads[i].wait()
 
     def normed_of(raw):
@@ -348,11 +359,11 @@
         own_o[1, pl.ds(pair * PAIR, PAIR), :] = unpaired(mixed, tokens)
     self_top, self_amount = split_heads(tops), split_heads(amounts)
 
-    for i in range(8, len(loads)):
+    for i in range(10, len(loads)):
         loads[i].wait()
     for copy in part_copies:
         copy.wait()
-    for copy in (to_next, to_far, *sides, *forwards):
+    for copy in (to_prev, to_next, to_far, *sides, *forwards):
         copy.wait_send()
 
     all_tops = [own_top, self_top] + [st_recv[i, pl.ds(0, HEADS), :] for i in range(3)]
@@ -405,13 +416,15 @@
     keys = coarse_flat.shape[0]
     gain1 = attn_gain.reshape(1, width)
     gain2 = mlp_gain.reshape(1, width)
-    smem = pl.BlockSpec(memory_space=pltpu.SMEM)
     anywhere = pl.BlockSpec(memory_space=pltpu.HBM)
 
     def room(like):
         return pltpu.VMEM(like.shape, like.dtype)
 
-    operands = (
+    small = tuple(
+        pltpu.with_memory_space_constraint(x, pltpu.HBM) for x in (block_table, shifts)
+    )
+    operands = tuple(pltpu.with_memory_space_constraint(x, pltpu.HBM) for x in (
         flat,
         coarse_flat,
         gain1,
@@ -425,12 +438,12 @@
         w_gate,
         w_up,
         w_down,
-    )
+    ))
     flops = 2 * keys * coarse.shape[-1] * 2 * width + 6 * tokens * width * w_gate.shape[-1]
     result = pl.pallas_call(
         functools.partial(kernel, tiles, narrows),
-        out_shape=jax.ShapeDtypeStruct((tokens, width), fine.dtype),
-        in_specs=[smem, smem] + [anywhere] * len(operands),
+        out_shape=pltpu.VMEM((tokens, width), fine.dtype),
+        in_specs=[anywhere] * (2 + len(operands)),
         out_specs=pl.BlockSpec(memory_space=pltpu.VMEM),
         scratch_shapes=[
             pltpu.VMEM(((7 if narrows > 2 else 5) * tokens, width), BF16),
@@ -447,17 +460,19 @@
             pltpu.VMEM((3, width, tokens), BF16),
             pltpu.VMEM((3, 2 * HEADS, tokens), F32),
             pltpu.VMEM((2, width, tokens), F32),
-            pltpu.SemaphoreType.DMA((len(operands),)),
+            pltpu.SMEM(block_table.shape, jnp.int32),
+            pltpu.SMEM(shifts.shape, jnp.int32),
+            pltpu.SemaphoreType.DMA((2 + len(operands),)),
             pltpu.SemaphoreType.DMA((17,)),
             pltpu.SemaphoreType.DMA((17,)),
         ],
         compiler_params=pltpu.CompilerParams(
-            collective_id=0, has_side_effects=True, vmem_limit_bytes=60 * 1024 * 1024
+            collective_id=0, has_side_effects=True, vmem_limit_bytes=56 * 1024 * 1024
         ),
         cost_estimate=pl.CostEstimate(
             flops=flops, bytes_accessed=12 * 1024 * 1024, transcendentals=2 * 1024 * 1024
         ),
-    )(block_table, shifts, *operands)
+    )(*small, *operands)
     return result.reshape(fine.shape)
 
 

time: 28.5 us -> 28.7 us (level)
  Pallas kernels: 26.8 us -> 27.9 us
  local copies, waits for them, and re-layouts: 1.57 us -> 0.66 us
    pallas_call x1, Pallas kernels: 26.8 us -> 27.9 us  [local(): pl.pallas_call(functools.partial(kernel, tiles, narrows), out_shape=pltpu...]
    unnamed x1, local copies, waits for them, and re-layouts: 1.57 us -> 0.66 us
where the time goes in v4:
time: 28.7 us; the launch traced here: 28.6 us
  Pallas kernels  27.9 us (97%)
  local copies, waits for them, and re-layouts  0.66 us (2%)
    pallas_call x1, Pallas kernels, local(): pl.pallas_call(functools.partial(kernel, tiles, narrows), out_shape=pltpu...  27.9 us
    unnamed x1, local copies, waits for them, and re-layouts  0.66 us

profile of v4, /device:TPU:0, one launch (start us, length us, event | category | flops | bytes accessed | tf_op | source)
XLA Modules:
  0.0 28.6 jit_solution(10002651747784222265)
XLA Ops:
  0.0 27.9 %shard_map.145 = bf16[128,512]{1,0:T(8,128)(2,1)S(1)} custom-call(s32[1,8]{1,0:T(1,128)} %table_in.1, s32[2]{0:T(128)} %shifts_in.1, bf16[128,512]{1,0:T(8,128)(2,1)} %bitcast.7, bf16[512,1024]{1,0:T(8,128)(2,1)} %bitcast.6, f32[1,512]{1,0:T(1,128)} %bitcast.8, bf16[512,512]{1,0:T(8,128)(2,1)} %w_query.1, bf16[512,512]{1,0:T(8,128)(2,1)} %w_key.1, ...), custom_call_target="tpu_custom_call" | custom-call | flops 1879048192 | bytes 12582912 | tf_op jit(solution)/shard_map/pallas_call | solution.py:443
  27.9 0.7 %copy.17 = bf16[16,8,512]{2,1,0:T(8,128)(2,1)} copy(bf16[16,8,512]{2,1,0:T(8,128)(2,1)S(1)} %bitcast.5) | data formatting | bytes 262144

commit v5 on v4

--- a/solution.py
+++ b/solution.py
@@ -87,6 +87,10 @@
     o_recv,
     st_recv,
     own_o,
+    far_send,
+    far_recv,
+    far_st_send,
+    far_st_recv,
     table,
     shifts,
     load_sem,
@@ -150,13 +154,18 @@
 
     above, below, side, other = tokens, 2 * tokens, 3 * tokens, 5 * tokens
     pl.semaphore_wait(barrier, 6)
-    to_prev = remote(2, fine, ext.at[pl.ds(below, tokens)], (s_prev, n))
-    to_next = remote(3, fine, ext.at[pl.ds(above, tokens)], (s_next, n))
+    even = lax.rem(s, 2) == 0
+    peer_a = jnp.where(even, s_prev, s_next)
+    peer_b = jnp.where(even, s_next, s_prev)
+    at_a = pl.multiple_of(jnp.where(even, above, below), half)
+    at_b = pl.multiple_of(jnp.where(even, below, above), half)
+    to_a = remote(2, fine, ext.at[pl.ds(at_b, tokens)], (peer_a, n))
+    to_b = remote(3, fine, ext.at[pl.ds(at_a, tokens)], (peer_b, n))
     to_far = remote(4, fine.at[pl.ds(0, half)], far, (s_prev2, n))
     sides = [remote(5, fine, ext.at[pl.ds(side, tokens)], (s, n_prev))]
     if two_sides:
         sides.append(remote(6, fine, ext.at[pl.ds(other, tokens)], (s, n_next)))
-    for copy in (to_far, to_prev, *sides):
+    for copy in (to_far, to_a, *sides):
         copy.start()
     for i in range(8, len(loads)):
         loads[i].start()
@@ -197,7 +206,7 @@
         loads[i].wait()
     keys_v[...] = dot(coarse_v[...], ck_v[...]).astype(BF16)
     values_t[...] = dot(coarse_v[...], cv_v[...]).T.astype(BF16)
-    to_next.start()
+    to_b.start()
 
     for i in range(5, 10):
         loads[i].wait()
@@ -225,9 +234,9 @@
     by_next = [table_recv[1, pl.ds(b, 1), :] for b in range(blocks)]
     by_none = [HIDDEN] * blocks
 
-    def attend(pair, q_t, biases):
+    def attend(pair, q_pair, biases):
         at = slice(pair * PAIR, (pair + 1) * PAIR)
-        scores = dot(keys_v[:, at], paired(q_t[at]))
+        scores = dot(keys_v[:, at], q_pair)
         parts = [scores[b * CT : (b + 1) * CT] for b in range(blocks)]
         top = None
         for part, hide in zip(parts, biases):
@@ -240,7 +249,7 @@
         ]
         amount = sum(jnp.sum(part, axis=0, keepdims=True) for part in parts)
         mixed = dot(values_t[at, :], jnp.concatenate(parts, axis=0).astype(BF16))
-        return top, amount, unpaired(mixed, tokens)
+        return top, amount, mixed
 
     def split_heads(rows):
         halves = []
@@ -251,8 +260,9 @@
     def cross(q_t, biases, store):
         tops, amounts = [], []
         for pair in range(HEADS // 2):
-            top, amount, mixed = attend(pair, q_t, biases)
-            store(pair, mixed)
+            q_pair = paired(q_t[pair * PAIR : (pair + 1) * PAIR])
+            top, amount, mixed = attend(pair, q_pair, biases)
+            store(pair, unpaired(mixed, tokens))
             tops.append(top)
             amounts.append(amount)
         return split_heads(tops), split_heads(amounts)
@@ -278,35 +288,72 @@
     forwards = []
 
     def forward(slot, at, place):
-        src = ext.at[pl.ds(at, half)]
-        copies = [remote(slot, src, ext.at[pl.ds(side + place, half)], (s, n_prev))]
+        src = ext.at[pl.ds(pl.multiple_of(at, half), half)]
+        dst = ext.at[pl.ds(pl.multiple_of(side + place, half), half)]
+        copies = [remote(slot, src, dst, (s, n_prev))]
         if two_sides:
-            copies.append(
-                remote(slot + 1, src, ext.at[pl.ds(other + place, half)], (s, n_next))
-            )
+            dst = ext.at[pl.ds(pl.multiple_of(other + place, half), half)]
+            copies.append(remote(slot + 1, src, dst, (s, n_next)))
         for copy in copies:
             copy.start()
         return copies
 
+    lane = lax.broadcasted_iota(jnp.int32, (1, tokens), 1)
+    left_half = lane < half
+    far_early = ((lane & (half - 1)) >> 3) < shift_row
+    far_bias = [jnp.where(far_early, x, HIDDEN) for x in by_next]
+    quadrant = (lax.broadcasted_iota(jnp.int32, (PAIR, tokens), 0) < HD) == (
+        lax.broadcasted_iota(jnp.int32, (PAIR, tokens), 1) < half
+    )
+    quadrant = jnp.where(quadrant, 1.0, 0.0).astype(BF16)
     to_far.wait_recv()
     far_raw = far[...]
-    part_copies = neighbour(
-        2,
-        jnp.concatenate([far_raw, far_raw], axis=0),
-        token_bias(by_next, by_none),
-        (s_next2, n),
-    )
-    to_prev.wait_recv()
-    forwards += forward(13, below, tokens + half)
+    far_q = queries_of(jnp.concatenate([far_raw, far_raw], axis=0))
+    tops, amounts = [], []
+    for pair in range(HEADS // 2):
+        at = slice(pair * PAIR, (pair + 1) * PAIR)
+        top, amount, mixed = attend(pair, far_q[at] * quadrant, far_bias)
+        far_send[pl.ds(pair * HD, HD), :] = jnp.where(left_half, mixed[:HD], mixed[HD:]).astype(
+            BF16
+        )
+        tops.append(top)
+        amounts.append(amount)
+    far_st_send[...] = jnp.concatenate(tops + amounts, axis=0)
+    part_copies = [
+        remote(11, far_st_send, far_st_recv, (s_next2, n)),
+        remote(12, far_send, far_recv, (s_next2, n)),
+    ]
+    for copy in part_copies:
+        copy.start()
+
+    def choose(x, y):
+        return [jnp.where(even, a, b) for a, b in zip(x, y)]
+
+    last_above, first_below = above + tokens - half, below
+    to_a.wait_recv()
+    forwards += forward(
+        13,
+        jnp.where(even, last_above, first_below),
+        jnp.where(even, tokens, tokens + half),
+    )
     part_copies += neighbour(
-        0, ext[pl.ds(below, tokens), :], token_bias(by_own, by_next), (s_next, n)
-    )
-    to_next.wait_recv()
-    forwards += forward(15, above + tokens - half, tokens)
+        0,
+        ext[pl.ds(at_a, tokens), :],
+        token_bias(choose(by_none, by_own), choose(by_prev, by_next)),
+        (peer_a, n),
+    )
+    to_b.wait_recv()
+    forwards += forward(
+        15,
+        jnp.where(even, first_below, last_above),
+        jnp.where(even, tokens + half, tokens),
+    )
     part_copies += neighbour(
-        1, ext[pl.ds(above, tokens), :], token_bias(by_none, by_prev), (s_prev, n)
-    )
-
+        1,
+        ext[pl.ds(at_b, tokens), :],
+        token_bias(choose(by_own, by_none), choose(by_next, by_prev)),
+        (peer_b, n),
+    )
     own_q = queries_of(ext[pl.ds(0, tokens), :])
     own_top, own_amount = cross(own_q, token_bias(by_prev, by_own), keep)
 
@@ -363,13 +410,26 @@
         loads[i].wait()
     for copy in part_copies:
         copy.wait()
-    for copy in (to_prev, to_next, to_far, *sides, *forwards):
+    for copy in (to_a, to_b, to_far, *sides, *forwards):
         copy.wait_send()
 
-    all_tops = [own_top, self_top] + [st_recv[i, pl.ds(0, HEADS), :] for i in range(3)]
+    def swapped(x):
+        return jnp.concatenate([x[:, half:], x[:, :half]], axis=1)
+
+    def far_rows(first, absent):
+        straight = far_st_recv[pl.ds(first, HEADS // 2), :]
+        crossed = swapped(straight)
+        rows = []
+        for i in range(HEADS // 2):
+            rows += [straight[i : i + 1], crossed[i : i + 1]]
+        return jnp.where(left_half, jnp.concatenate(rows, axis=0), absent)
+
+    all_tops = [own_top, self_top] + [st_recv[i, pl.ds(0, HEADS), :] for i in range(2)]
+    all_tops.append(far_rows(0, HIDDEN))
     all_amounts = [own_amount, self_amount] + [
-        st_recv[i, pl.ds(HEADS, HEADS), :] for i in range(3)
+        st_recv[i, pl.ds(HEADS, HEADS), :] for i in range(2)
     ]
+    all_amounts.append(far_rows(HEADS // 2, 0.0))
     top = functools.reduce(jnp.maximum, all_tops)
     scales = [jnp.exp(x - top) for x in all_tops]
     amount = sum(a * b for a, b in zip(scales, all_amounts))
@@ -378,7 +438,11 @@
     for h in range(HEADS):
         at = pl.ds(h * HD, HD)
         mixed = own_o[0, at, :] * scales[0][h : h + 1] + own_o[1, at, :] * scales[1][h : h + 1]
-        for i in range(3):
+        distant = far_recv[pl.ds(h // 2 * HD, HD), :].astype(F32)
+        if h % 2:
+            distant = swapped(distant)
+        mixed = mixed + distant * scales[4][h : h + 1]
+        for i in range(2):
             mixed = mixed + o_recv[i, at, :].astype(F32) * scales[2 + i][h : h + 1]
         heads.append(mixed)
     head_out = jnp.concatenate(heads, axis=0).T.astype(BF16)
@@ -455,11 +519,15 @@
             pltpu.VMEM((width, keys), BF16),
             pltpu.VMEM((16, tokens), F32),
             pltpu.VMEM((2, 8, tokens), F32),
-            pltpu.VMEM((3, width, tokens), BF16),
-            pltpu.VMEM((3, 2 * HEADS, tokens), F32),
-            pltpu.VMEM((3, width, tokens), BF16),
-            pltpu.VMEM((3, 2 * HEADS, tokens), F32),
+            pltpu.VMEM((2, width, tokens), BF16),
+            pltpu.VMEM((2, 2 * HEADS, tokens), F32),
+            pltpu.VMEM((2, width, tokens), BF16),
+            pltpu.VMEM((2, 2 * HEADS, tokens), F32),
             pltpu.VMEM((2, width, tokens), F32),
+            pltpu.VMEM((width // 2, tokens), BF16),
+            pltpu.VMEM((width // 2, tokens), BF16),
+            pltpu.VMEM((HEADS, tokens), F32),
+            pltpu.VMEM((HEADS, tokens), F32),
             pltpu.SMEM(block_table.shape, jnp.int32),
             pltpu.SMEM(shifts.shape, jnp.int32),
             pltpu.SemaphoreType.DMA((2 + len(operands),)),

time: 28.7 us -> 26.7 us (0.930)
  Pallas kernels: 27.9 us -> 25.9 us
    pallas_call x1, Pallas kernels: 27.9 us -> 25.9 us  [local(): pl.pallas_call(functools.partial(kernel, tiles, narrows), out_shape=pltpu...]
where the time goes in v5:
time: 26.7 us; the launch traced here: 26.5 us
  Pallas kernels  25.9 us (97%)
  local copies, waits for them, and re-layouts  0.66 us (2%)
    pallas_call x1, Pallas kernels, local(): pl.pallas_call(functools.partial(kernel, tiles, narrows), out_shape=pltpu...  25.9 us
    unnamed x1, local copies, waits for them, and re-layouts  0.66 us

profile of v5, /device:TPU:0, one launch (start us, length us, event | category | flops | bytes accessed | tf_op | source)
XLA Modules:
  0.0 26.5 jit_solution(11257719489483665350)
XLA Ops:
  0.0 25.9 %shard_map.145 = bf16[128,512]{1,0:T(8,128)(2,1)S(1)} custom-call(s32[1,8]{1,0:T(1,128)} %table_in.1, s32[2]{0:T(128)} %shifts_in.1, bf16[128,512]{1,0:T(8,128)(2,1)} %bitcast.7, bf16[512,1024]{1,0:T(8,128)(2,1)} %bitcast.6, f32[1,512]{1,0:T(1,128)} %bitcast.8, bf16[512,512]{1,0:T(8,128)(2,1)} %w_query.1, bf16[512,512]{1,0:T(8,128)(2,1)} %w_key.1, ...), custom_call_target="tpu_custom_call" | custom-call | flops 1879048192 | bytes 12582912 | tf_op jit(solution)/shard_map/pallas_call | solution.py:507
  25.9 0.7 %copy.17 = bf16[16,8,512]{2,1,0:T(8,128)(2,1)} copy(bf16[16,8,512]{2,1,0:T(8,128)(2,1)S(1)} %bitcast.5) | data formatting | bytes 262144

commit v6 on v5

--- a/solution.py
+++ b/solution.py
@@ -165,7 +165,7 @@
     sides = [remote(5, fine, ext.at[pl.ds(side, tokens)], (s, n_prev))]
     if two_sides:
         sides.append(remote(6, fine, ext.at[pl.ds(other, tokens)], (s, n_next)))
-    for copy in (to_far, to_a, *sides):
+    for copy in (to_a, to_far, *sides):
         copy.start()
     for i in range(8, len(loads)):
         loads[i].start()
@@ -298,6 +298,37 @@
             copy.start()
         return copies
 
+    own_q = queries_of(ext[pl.ds(0, tokens), :])
+    own_top, own_amount = cross(own_q, token_bias(by_prev, by_own), keep)
+
+    def choose(x, y):
+        return [jnp.where(even, a, b) for a, b in zip(x, y)]
+
+    last_above, first_below = above + tokens - half, below
+    to_a.wait_recv()
+    forwards += forward(
+        13,
+        jnp.where(even, last_above, first_below),
+        jnp.where(even, tokens, tokens + half),
+    )
+    part_copies = neighbour(
+        0,
+        ext[pl.ds(at_a, tokens), :],
+        token_bias(choose(by_none, by_own), choose(by_prev, by_next)),
+        (peer_a, n),
+    )
+    to_b.wait_recv()
+    forwards += forward(
+        15,
+        jnp.where(even, first_below, last_above),
+        jnp.where(even, tokens + half, tokens),
+    )
+    part_copies += neighbour(
+        1,
+        ext[pl.ds(at_b, tokens), :],
+        token_bias(choose(by_own, by_none), choose(by_next, by_prev)),
+        (peer_b, n),
+    )
     lane = lax.broadcasted_iota(jnp.int32, (1, tokens), 1)
     left_half = lane < half
     far_early = ((lane & (half - 1)) >> 3) < shift_row
@@ -319,43 +350,13 @@
         tops.append(top)
         amounts.append(amount)
     far_st_send[...] = jnp.concatenate(tops + amounts, axis=0)
-    part_copies = [
+    far_copies = [
         remote(11, far_st_send, far_st_recv, (s_next2, n)),
         remote(12, far_send, far_recv, (s_next2, n)),
     ]
-    for copy in part_copies:
+    for copy in far_copies:
         copy.start()
-
-    def choose(x, y):
-        return [jnp.where(even, a, b) for a, b in zip(x, y)]
-
-    last_above, first_below = above + tokens - half, below
-    to_a.wait_recv()
-    forwards += forward(
-        13,
-        jnp.where(even, last_above, first_below),
-        jnp.where(even, tokens, tokens + half),
-    )
-    part_copies += neighbour(
-        0,
-        ext[pl.ds(at_a, tokens), :],
-        token_bias(choose(by_none, by_own), choose(by_prev, by_next)),
-        (peer_a, n),
-    )
-    to_b.wait_recv()
-    forwards += forward(
-        15,
-        jnp.where(even, first_below, last_above),
-        jnp.where(even, tokens + half, tokens),
-    )
-    part_copies += neighbour(
-        1,
-        ext[pl.ds(at_b, tokens), :],
-        token_bias(choose(by_own, by_none), choose(by_next, by_prev)),
-        (peer_b, n),
-    )
-    own_q = queries_of(ext[pl.ds(0, tokens), :])
-    own_top, own_amount = cross(own_q, token_bias(by_prev, by_own), keep)
+    part_copies += far_copies
 
     for copy in sides:
         copy.wait_recv()

time: 26.7 us -> 28 us (1.049)
  Pallas kernels: 25.9 us -> 27.2 us
    pallas_call x1, Pallas kernels: 25.9 us -> 27.2 us  [local(): pl.pallas_call(functools.partial(kernel, tiles, narrows), out_shape=pltpu...]
where the time goes in v6:
time: 28 us; the launch traced here: 27.9 us
  Pallas kernels  27.2 us (97%)
  local copies, waits for them, and re-layouts  0.66 us (2%)
    pallas_call x1, Pallas kernels, local(): pl.pallas_call(functools.partial(kernel, tiles, narrows), out_shape=pltpu...  27.2 us
    unnamed x1, local copies, waits for them, and re-layouts  0.66 us

profile of v6, /device:TPU:0, one launch (start us, length us, event | category | flops | bytes accessed | tf_op | source)
XLA Modules:
  0.0 27.9 jit_solution(16410271455789272624)
XLA Ops:
  0.0 27.2 %shard_map.145 = bf16[128,512]{1,0:T(8,128)(2,1)S(1)} custom-call(s32[1,8]{1,0:T(1,128)} %table_in.1, s32[2]{0:T(128)} %shifts_in.1, bf16[128,512]{1,0:T(8,128)(2,1)} %bitcast.7, bf16[512,1024]{1,0:T(8,128)(2,1)} %bitcast.6, f32[1,512]{1,0:T(1,128)} %bitcast.8, bf16[512,512]{1,0:T(8,128)(2,1)} %w_query.1, bf16[512,512]{1,0:T(8,128)(2,1)} %w_key.1, ...), custom_call_target="tpu_custom_call" | custom-call | flops 1879048192 | bytes 12582912 | tf_op jit(solution)/shard_map/pallas_call | solution.py:508
  27.2 0.7 %copy.17 = bf16[16,8,512]{2,1,0:T(8,128)(2,1)} copy(bf16[16,8,512]{2,1,0:T(8,128)(2,1)S(1)} %bitcast.5) | data formatting | bytes 262144

commit v7 on v6

--- a/solution.py
+++ b/solution.py
@@ -205,8 +205,8 @@
     for i in range(3):
         loads[i].wait()
     keys_v[...] = dot(coarse_v[...], ck_v[...]).astype(BF16)
+    to_b.start()
     values_t[...] = dot(coarse_v[...], cv_v[...]).T.astype(BF16)
-    to_b.start()
 
     for i in range(5, 10):
         loads[i].wait()
@@ -297,9 +297,6 @@
         for copy in copies:
             copy.start()
         return copies
-
-    own_q = queries_of(ext[pl.ds(0, tokens), :])
-    own_top, own_amount = cross(own_q, token_bias(by_prev, by_own), keep)
 
     def choose(x, y):
         return [jnp.where(even, a, b) for a, b in zip(x, y)]
@@ -357,6 +354,9 @@
     for copy in far_copies:
         copy.start()
     part_copies += far_copies
+
+    own_q = queries_of(ext[pl.ds(0, tokens), :])
+    own_top, own_amount = cross(own_q, token_bias(by_prev, by_own), keep)
 
     for copy in sides:
         copy.wait_recv()

time: 28 us -> 26.5 us (0.946)
  Pallas kernels: 27.2 us -> 25.7 us
    pallas_call x1, Pallas kernels: 27.2 us -> 25.7 us  [local(): pl.pallas_call(functools.partial(kernel, tiles, narrows), out_shape=pltpu...]
where the time goes in v7:
time: 26.5 us; the launch traced here: 26.3 us
  Pallas kernels  25.7 us (97%)
  local copies, waits for them, and re-layouts  0.66 us (2%)
    pallas_call x1, Pallas kernels, local(): pl.pallas_call(functools.partial(kernel, tiles, narrows), out_shape=pltpu...  25.7 us
    unnamed x1, local copies, waits for them, and re-layouts  0.66 us

profile of v7, /device:TPU:0, one launch (start us, length us, event | category | flops | bytes accessed | tf_op | source)
XLA Modules:
  0.0 26.3 jit_solution(15564294711998997624)
XLA Ops:
  0.0 25.7 %shard_map.145 = bf16[128,512]{1,0:T(8,128)(2,1)S(1)} custom-call(s32[1,8]{1,0:T(1,128)} %table_in.1, s32[2]{0:T(128)} %shifts_in.1, bf16[128,512]{1,0:T(8,128)(2,1)} %bitcast.7, bf16[512,1024]{1,0:T(8,128)(2,1)} %bitcast.6, f32[1,512]{1,0:T(1,128)} %bitcast.8, bf16[512,512]{1,0:T(8,128)(2,1)} %w_query.1, bf16[512,512]{1,0:T(8,128)(2,1)} %w_key.1, ...), custom_call_target="tpu_custom_call" | custom-call | flops 1879048192 | bytes 12582912 | tf_op jit(solution)/shard_map/pallas_call | solution.py:508
  25.7 0.7 %copy.17 = bf16[16,8,512]{2,1,0:T(8,128)(2,1)} copy(bf16[16,8,512]{2,1,0:T(8,128)(2,1)S(1)} %bitcast.5) | data formatting | bytes 262144
